TPU v7x, 256 devices: a whole 4x4x8 slice. The times are simulated.
256 devices in a mesh: dp: 4 (over z_lo), seq: 64 (over y, x, z_hi, core).
Axes of the slice: x: 4, y: 4, z: 8 (z_hi: 2, z_lo: 4; z = z_hi * 4 + z_lo), core: 2. Of those that a mesh axis runs over, the one named last changes fastest.
Arguments:
- grad_out: bfloat16 [4, 8192, 4096], P('dp', 'seq'), may hold values from -6 to 6
- query_proj: bfloat16 [4, 8192, 4096], P('dp', 'seq'), may hold values from -6 to 6
- key_proj: bfloat16 [4, 8192, 4096], P('dp', 'seq'), may hold values from -6 to 6
- value_proj: bfloat16 [4, 8192, 4096], P('dp', 'seq'), may hold values from -6 to 6
- conv_out: bfloat16 [4, 8192, 4096], P('dp', 'seq'), may hold values from -6 to 6
- filters: float32 [4096, 8192], P('seq'), may hold values from -0.0625 to 0.0625
Outputs:
- grad_query: bfloat16 [4, 8192, 4096], P('dp', 'seq')
- grad_key: bfloat16 [4, 8192, 4096], P('dp', 'seq')
- grad_value: bfloat16 [4, 8192, 4096], P('dp', 'seq')
- filter_grad: float32 [4096, 8192], P('seq', 'dp')
All inputs are finite; a program needn't handle non-finite values.
Results may differ from a plain program's by a relative error of at most 0.0058.
Values may be sent and summed in bfloat16 or wider, within the bound.
A program may use at most 128 MiB of HBM per device.

v0:
```python
import math

import jax
import jax.numpy as jnp
from jax import lax
from jax.sharding import PartitionSpec as P


def make_tables(seq_count, tok_rows):
    two_q = 2 * seq_count
    size_fft = two_q * tok_rows
    freq_index = lax.iota(jnp.int32, seq_count + 1)
    block_index = lax.iota(jnp.int32, seq_count)
    row_index = lax.iota(jnp.int32, tok_rows)
    angle_first = (
        2.0
        * math.pi
        / two_q
        * (freq_index[:, None] * block_index[None, :] % two_q).astype(jnp.float32)
    )
    angle_second = (
        2.0
        * math.pi
        / tok_rows
        * (row_index[:, None] * row_index[None, :] % tok_rows).astype(jnp.float32)
    )
    angle_twist = (
        2.0
        * math.pi
        / size_fft
        * (freq_index[:, None] * row_index[None, :] % size_fft).astype(jnp.float32)
    )
    edge = (freq_index == 0) | (freq_index == seq_count)
    weights = jnp.where(edge, 1.0, 2.0).astype(jnp.float32)[:, None]
    cos_first = jnp.cos(angle_first)
    sin_first = jnp.sin(angle_first)
    return (
        cos_first,
        sin_first,
        jnp.cos(angle_second),
        jnp.sin(angle_second),
        jnp.cos(angle_twist)[:, None, :],
        jnp.sin(angle_twist)[:, None, :],
        cos_first * weights,
        sin_first * weights,
        float(size_fft),
    )


def along_rows(spectrum, matrix):
    return jnp.einsum("kcr,rm->kcm", spectrum, matrix, precision=lax.Precision.HIGHEST)


def forward(signal_in, tables):
    cos_first, sin_first, cos_second, sin_second, twist_cos, twist_sin = tables[:6]
    values = signal_in.astype(jnp.float32)
    first_re = jnp.einsum("ka,acr->kcr", cos_first, values, precision=lax.Precision.HIGHEST)
    first_im = -jnp.einsum("ka,acr->kcr", sin_first, values, precision=lax.Precision.HIGHEST)
    turned_re = first_re * twist_cos + first_im * twist_sin
    turned_im = first_im * twist_cos - first_re * twist_sin
    out_re = along_rows(turned_re, cos_second) + along_rows(turned_im, sin_second)
    out_im = along_rows(turned_im, cos_second) - along_rows(turned_re, sin_second)
    return (out_re, out_im)


def inverse(spec_re, spec_im, tables):
    cos_second, sin_second, twist_cos, twist_sin = tables[2:6]
    back_cos, back_sin, size_fft = (tables[6], tables[7], tables[8])
    inner_re = along_rows(spec_re, cos_second) - along_rows(spec_im, sin_second)
    inner_im = along_rows(spec_im, cos_second) + along_rows(spec_re, sin_second)
    turned_re = inner_re * twist_cos - inner_im * twist_sin
    turned_im = inner_im * twist_cos + inner_re * twist_sin
    result = jnp.einsum("ka,kcr->acr", back_cos, turned_re, precision=lax.Precision.HIGHEST)
    result = result - jnp.einsum(
        "ka,kcr->acr", back_sin, turned_im, precision=lax.Precision.HIGHEST
    )
    return result / size_fft


def local(grad_out, query_proj, key_proj, value_proj, conv_out, filters):
    seq_count = lax.axis_size("seq")
    dp_count = lax.axis_size("dp")
    tok_rows = grad_out.shape[1]
    channels = grad_out.shape[2]
    group_width = channels // seq_count
    seq_length = tok_rows * seq_count
    tables = make_tables(seq_count, tok_rows)
    grad_rows = grad_out[0].astype(jnp.float32)
    grad_query = (grad_rows * conv_out[0].astype(jnp.float32)).astype(jnp.bfloat16)[None]
    product = (key_proj[0].astype(jnp.float32) * value_proj[0].astype(jnp.float32)).astype(
        jnp.bfloat16
    )
    signal = (grad_rows * query_proj[0].astype(jnp.float32)).astype(jnp.bfloat16)

    def blocks(matrix):
        return matrix.T.reshape(seq_count, group_width, tok_rows)

    prod_re, prod_im = forward(
        lax.all_to_all(blocks(product), "seq", split_axis=0, concat_axis=0, tiled=True), tables
    )
    sig_re, sig_im = forward(
        lax.all_to_all(blocks(signal), "seq", split_axis=0, concat_axis=0, tiled=True), tables
    )
    prod_re, prod_im, sig_re, sig_im = (prod_re, prod_im, sig_re, sig_im)
    filt_time = jnp.transpose(filters.reshape(group_width, seq_count, tok_rows), (1, 0, 2))
    filt_re, filt_im = forward(filt_time, tables)
    corr_time = inverse(
        filt_re * sig_re + filt_im * sig_im, filt_re * sig_im - filt_im * sig_re, tables
    )
    returned = lax.all_to_all(
        corr_time.astype(jnp.bfloat16), "seq", split_axis=0, concat_axis=0, tiled=True
    )
    grad_prod = returned.reshape(channels, tok_rows).T.astype(jnp.float32)
    grad_key = (grad_prod * value_proj[0].astype(jnp.float32)).astype(jnp.bfloat16)[None]
    grad_value = (grad_prod * key_proj[0].astype(jnp.float32)).astype(jnp.bfloat16)[None]
    cross_re = prod_re * sig_re + prod_im * sig_im
    cross_im = prod_re * sig_im - prod_im * sig_re
    summed_re, summed_im = (
        lax.psum_scatter(cross_re, "dp", scatter_dimension=1, tiled=True),
        lax.psum_scatter(cross_im, "dp", scatter_dimension=1, tiled=True),
    )
    local_taps = inverse(summed_re, summed_im, tables)
    taps_mine = lax.all_to_all(local_taps, "dp", split_axis=0, concat_axis=1, tiled=True)
    scale = 1.0 / math.sqrt(dp_count * seq_length)
    filter_grad = jnp.transpose(taps_mine, (1, 0, 2)).reshape(group_width, -1) * scale
    return (grad_query, grad_key, grad_value, filter_grad)


def solution(mesh):
    in_specs = (
        P("dp", "seq", None),
        P("dp", "seq", None),
        P("dp", "seq", None),
        P("dp", "seq", None),
        P("dp", "seq", None),
        P("seq", None),
    )
    out_specs = (P("dp", "seq", None), P("dp", "seq", None), P("dp", "seq", None), P("seq", "dp"))
    return jax.shard_map(local, mesh=mesh, in_specs=in_specs, out_specs=out_specs, check_vma=False)
```

profile of v0, /device:TPU:1, one launch (start us, length us, event | category | flops | bytes accessed | tf_op | source)
XLA Modules:
  0.0 285.9 jit_solution(13812714693278063470)
XLA Ops:
  7.2 0.0 copy-start.9
  7.2 1.7 copy.122
  8.9 0.7 copy.123
  9.6 1.6 copy.126
  11.2 1.8 fusion.17
  13.0 15.7 %all-to-all-start = ((bf16[64,64,128]{2,1,0:T(8,128)(2,1)}), bf16[64,64,128]{2,1,0:T(8,128)(2,1)S(1)}, u32[]{:S(2)}, u32[]{:S(2)}) async-start(bf16[64,64,128]{2,1,0:T(8,128)(2,1)} %bitcast.8), calls=%async_computation | async-start | bytes 2097152 | tf_op jit(solution)/shard_map/all_to_all | solution.py:102
  28.7 0.7 copy.140
  29.4 1.6 copy.141
  31.1 1.3 fusion.20
  32.4 21.2 %all-to-all-done = bf16[64,64,128]{2,1,0:T(8,128)(2,1)S(1)} async-done(((bf16[64,64,128]{2,1,0:T(8,128)(2,1)}), bf16[64,64,128]{2,1,0:T(8,128)(2,1)S(1)}, u32[]{:S(2)}, u32[]{:S(2)}) %all-to-all-start) | async-done | bytes 1048608 | tf_op jit(solution)/shard_map/all_to_all | solution.py:102
  53.5 7.4 %all-to-all-start.2 = ((bf16[64,64,128]{2,1,0:T(8,128)(2,1)}), bf16[64,64,128]{2,1,0:T(8,128)(2,1)}, u32[]{:S(2)}, u32[]{:S(2)}) async-start(bf16[64,64,128]{2,1,0:T(8,128)(2,1)} %bitcast.129), calls=%async_computation.2 | async-start | bytes 2097152 | tf_op jit(solution)/shard_map/all_to_all | solution.py:99
  60.9 0.3 reduce-scatter.5.cloned.1.call-start
  61.3 2.0 copy.163
  63.3 0.2 fusion.169
  63.4 2.2 fusion.21
  65.7 0.0 copy-start.5
  65.7 3.6 %fusion.23 = f32[65,64,128]{2,0,1:T(8,128)} fusion(f32[64,64,128]{2,1,0:T(8,128)S(1)} %bitcast.128), kind=kOutput, calls=%fused_computation.39 | convolution fusion | flops 409002880 | bytes 4227072 | tf_op jit(solution)/shard_map/ka,acr->kcr/dot_general | solution.py:57
  69.3 3.0 %fusion.86 = f32[65,64,128]{2,0,1:T(8,128)} fusion(bf16[64,64,128]{2,1,0:T(8,128)(2,1)S(1)} %copy-done.5), kind=kOutput, calls=%fused_computation.88 | convolution fusion | flops 409002880 | bytes 3178496 | tf_op jit(solution)/shard_map/ka,acr->kcr/dot_general | solution.py:58
  72.3 3.0 %fusion.88 = f32[65,64,128]{2,0,1:T(8,128)} fusion(bf16[64,64,128]{2,1,0:T(8,128)(2,1)S(1)} %copy-done.5), kind=kOutput, calls=%fused_computation.90 | convolution fusion | flops 409002880 | bytes 3178496 | tf_op jit(solution)/shard_map/ka,acr->kcr/dot_general | solution.py:57
  75.4 7.8 %all-to-all-done.2 = bf16[64,64,128]{2,1,0:T(8,128)(2,1)} async-done(((bf16[64,64,128]{2,1,0:T(8,128)(2,1)}), bf16[64,64,128]{2,1,0:T(8,128)(2,1)}, u32[]{:S(2)}, u32[]{:S(2)}) %all-to-all-start.2) | async-done | bytes 1048608 | tf_op jit(solution)/shard_map/all_to_all | solution.py:99
  83.2 3.0 %fusion.82 = f32[65,64,128]{2,0,1:T(8,128)S(1)} fusion(bf16[64,64,128]{2,1,0:T(8,128)(2,1)} %all-to-all-done.2), kind=kOutput, calls=%fused_computation.84 | convolution fusion | flops 409002880 | bytes 3178496 | tf_op jit(solution)/shard_map/ka,acr->kcr/dot_general | solution.py:58
  86.2 6.5 %multiply_add_fusion = (f32[65,64,128]{2,0,1:T(8,128)S(1)}, f32[65,64,128]{2,0,1:T(8,128)S(1)}, f32[65,64,128]{2,0,1:T(8,128)S(1)}, f32[65,64,128]{2,0,1:T(8,128...) fusion(f32[65,64,128]{2,0,1:T(8,128)S(1)} %fusion.82, f32[65,128]{1,0:T(8,128)S(1)} %get-tuple-element.42, ...), kind=kOutput, calls=%fused_computation.6 | convolution fusion | flops 420184960 | bytes 24544256 | tf_op jit(solution)/shard_map/ka,acr->kcr/dot_general | solution.py:57
  92.7 2.2 fusion.43
  94.9 2.2 fusion.41
  97.1 2.2 fusion.35
  99.2 2.2 fusion.33
  101.4 2.2 fusion.27
  103.6 2.4 fusion.25
  106.0 2.3 fusion.55
  108.3 2.2 fusion.58
  110.5 2.3 fusion.61
  112.8 2.2 fusion.64
  115.0 2.5 fusion.67
  117.5 5.2 %multiply_add_fusion.3 = (f32[65,64,128]{2,1,0:T(8,128)}, f32[65,64,128]{2,1,0:T(8,128)}, f32[65,64,128]{2,1,0:T(8,128)}, f32[65,64,128]{2,1,0:T(8,128)S(1)}) fusion(f32[65,64,128]{2,1,0:T(8,128)S(1)} %fusion.64, f32[65,64,128]{2,1,0:T(8,128)S(1)} %fusion.67, f32[65,64,128]{2,1,0:T(8,128)S(1)} %fusion.61, f32[65,64,128]{2,1,0:T(8,128)S(1)} %fusion.58, ...), kind=kOutput, calls=%fused_computation.28 | convolution fusion | flops 825040896 | bytes 23429120 | tf_op jit(solution)/shard_map/kcr,rm->kcm/dot_general | solution.py:51
  122.7 0.0 reduce-scatter.5.cloned.1.call-update
  122.7 0.0 reduce-scatter.3.cloned.1.call-start
  122.7 0.7 reduce-scatter.3.cloned.1.call-update
  123.5 5.4 %fusion.8 = f32[65,64,128]{2,0,1:T(8,128)S(1)} fusion(f32[65,64,128]{2,1,0:T(8,128)} %get-tuple-element.30), kind=kOutput, calls=%fused_computation.19 | convolution fusion | flops 818118656 | bytes 4259840 | tf_op jit(solution)/shard_map/kcr,rm->kcm/dot_general | solution.py:51
  128.9 3.7 %fusion.10 = f32[65,64,128]{2,0,1:T(8,128)S(1)} fusion(f32[65,64,128]{2,1,0:T(8,128)S(1)} %copy-done), kind=kOutput, calls=%fused_computation.21 | convolution fusion | flops 818118656 | bytes 4259840 | tf_op jit(solution)/shard_map/kcr,rm->kcm/dot_general | solution.py:51
  132.6 3.8 %fusion.52 = f32[65,64,128]{2,0,1:T(8,128)S(1)} fusion(f32[65,64,128]{2,0,1:T(8,128)S(1)} %fusion.8, f32[65,64,128]{2,1,0:T(8,128)S(1)} %get-tuple-element.31), kind=kOutput, calls=%fused_computation.67 | convolution fusion | flops 818651136 | bytes 6389760 | tf_op jit(solution)/shard_map/kcr,rm->kcm/dot_general | solution.py:51
  136.3 4.2 %fusion.49 = f32[65,64,128]{2,0,1:T(8,128)S(1)} fusion(f32[65,64,128]{2,0,1:T(8,128)S(1)} %fusion.10, f32[65,64,128]{2,1,0:T(8,128)S(1)} %get-tuple-element.31), kind=kOutput, calls=%fused_computation.66 | convolution fusion | flops 818651136 | bytes 6389760 | tf_op jit(solution)/shard_map/kcr,rm->kcm/dot_general | solution.py:51
  140.6 2.2 fusion
  142.8 2.3 multiply_convert_fusion
  145.1 0.0 copy-start.6
  145.2 1.6 copy.139
  146.8 10.8 %all-to-all-start.1 = ((bf16[64,64,128]{2,1,0:T(8,128)(2,1)}), bf16[64,64,128]{2,1,0:T(8,128)(2,1)S(1)}, u32[]{:S(2)}, u32[]{:S(2)}) async-start(bf16[64,64,128]{2,1,0:T(8,128)(2,1)} %copy.139), calls=%async_computation.1 | async-start | bytes 2097152 | tf_op jit(solution)/shard_map/all_to_all | solution.py:110
  157.7 1.3 copy.153
  159.0 33.2 %reduce-scatter.5.cloned.1.call-done = f32[65,16,128]{2,1,0:T(8,128)} async-done(((f32[65,64,128]{2,1,0:T(8,128)}), f32[65,16,128]{2,1,0:T(8,128)}) %reduce-scatter.5.cloned.1.call-update) | async-done | bytes 532496 | tf_op jit(solution)/shard_map/reduce_scatter | solution.py:120
  192.1 1.9 fusion.106
  194.1 57.2 %reduce-scatter.3.cloned.1.call-done = f32[65,16,128]{2,1,0:T(8,128)} async-done(((f32[65,64,128]{2,1,0:T(8,128)}), f32[65,16,128]{2,1,0:T(8,128)}) %reduce-scatter.3.cloned.1.call-update) | async-done | bytes 532496 | tf_op jit(solution)/shard_map/reduce_scatter | solution.py:119
  251.3 1.9 fusion.108
  253.2 1.9 convolution_add_fusion
  255.1 0.9 multiply_add_fusion.5
  256.0 0.8 fusion.91
  256.8 0.8 fusion.75
  257.6 1.1 copy.150
  258.7 0.0 all-to-all-done.1
  258.7 4.1 %all-to-all-start.3 = ((f32[64,16,128]{2,1,0:T(8,128)}), f32[64,16,128]{2,1,0:T(8,128)}, u32[]{:S(2)}, u32[]{:S(2)}) async-start(f32[64,16,128]{2,1,0:T(8,128)} %copy.150), calls=%async_computation.5 | async-start | bytes 1048576 | tf_op jit(solution)/shard_map/all_to_all | solution.py:123
  262.9 1.9 fusion.81
  264.8 2.4 copy.154
  267.1 1.3 copy.155
  268.4 8.5 %all-to-all-done.3 = f32[64,16,128]{2,1,0:T(8,128)} async-done(((f32[64,16,128]{2,1,0:T(8,128)}), f32[64,16,128]{2,1,0:T(8,128)}, u32[]{:S(2)}, u32[]{:S(2)}) %all-to-all-start.3) | async-done | bytes 524320 | tf_op jit(solution)/shard_map/all_to_all | solution.py:123
  276.9 1.1 broadcast_multiply_fusion
  278.1 0.8 copy.229
  (21 shorter events, 0.1 us)
Async XLA Ops:
  7.2 1.7 copy-start.9
  13.0 15.8 %copy-start.10 = (bf16[1,128,4096]{2,1,0:T(8,128)(2,1)S(1)}, bf16[1,128,4096]{2,1,0:T(8,128)(2,1)}, u32[]{:S(2)}) copy-start(bf16[1,128,4096]{2,1,0:T(8,128)(2,1)} %param.9) | copy-start | bytes 3145732
  13.0 40.5 %all-to-all-start = ((bf16[64,64,128]{2,1,0:T(8,128)(2,1)}), bf16[64,64,128]{2,1,0:T(8,128)(2,1)S(1)}, u32[]{:S(2)}, u32[]{:S(2)}) async-start(bf16[64,64,128]{2,1,0:T(8,128)(2,1)} %bitcast.8), calls=%async_computation | async-start | bytes 2097152 | tf_op jit(solution)/shard_map/all_to_all | solution.py:102
  31.0 22.5 %copy-start.2 = (bf16[1,128,4096]{1,2,0:T(8,128)(2,1)}, bf16[1,128,4096]{1,2,0:T(8,128)(2,1)S(1)}, u32[]{:S(2)}) copy-start(bf16[1,128,4096]{1,2,0:T(8,128)(2,1)S(1)} %copy.141) | copy-start | bytes 3145732
  53.5 9.7 %copy-start.4 = (bf16[64,64,128]{2,1,0:T(8,128)(2,1)}, bf16[64,64,128]{2,1,0:T(8,128)(2,1)S(1)}, u32[]{:S(2)}) copy-start(bf16[64,64,128]{2,1,0:T(8,128)(2,1)S(1)} %all-to-all-done) | copy-start | bytes 3145732
  53.5 29.7 %all-to-all-start.2 = ((bf16[64,64,128]{2,1,0:T(8,128)(2,1)}), bf16[64,64,128]{2,1,0:T(8,128)(2,1)}, u32[]{:S(2)}, u32[]{:S(2)}) async-start(bf16[64,64,128]{2,1,0:T(8,128)(2,1)} %bitcast.129), calls=%async_computation.2 | async-start | bytes 2097152 | tf_op jit(solution)/shard_map/all_to_all | solution.py:99
  60.9 131.2 %reduce-scatter.5.cloned.1.call-start = ((), (), s32[]{:S(2)}) async-start(), calls=%async_computation.7 | async-start | bytes 2662400 | tf_op jit(solution)/shard_map/reduce_scatter | solution.py:120
  65.7 3.7 %copy-start.5 = (bf16[64,64,128]{2,1,0:T(8,128)(2,1)S(1)}, bf16[64,64,128]{2,1,0:T(8,128)(2,1)}, u32[]{:S(2)}) copy-start(bf16[64,64,128]{2,1,0:T(8,128)(2,1)} %copy-done.4) | copy-start | bytes 3145732
  83.2 3.0 %copy-start.1 = (f32[65,64,128]{2,0,1:T(8,128)S(1)}, f32[65,64,128]{2,0,1:T(8,128)}, u32[]{:S(2)}) copy-start(f32[65,64,128]{2,0,1:T(8,128)} %fusion.23) | copy-start | bytes 6389764
  122.7 128.6 %reduce-scatter.3.cloned.1.call-start = ((), (), s32[]{:S(2)}) async-start(), calls=%async_computation.6 | async-start | bytes 2662400 | tf_op jit(solution)/shard_map/reduce_scatter | solution.py:119
  123.5 5.4 %copy-start = (f32[65,64,128]{2,1,0:T(8,128)S(1)}, f32[65,64,128]{2,1,0:T(8,128)}, u32[]{:S(2)}) copy-start(f32[65,64,128]{2,1,0:T(8,128)} %get-tuple-element.30) | copy-start | bytes 6389764
  145.1 12.5 %copy-start.6 = (bf16[1,128,4096]{1,2,0:T(8,128)(2,1)S(1)}, bf16[1,128,4096]{1,2,0:T(8,128)(2,1)}, u32[]{:S(2)}) copy-start(bf16[1,128,4096]{1,2,0:T(8,128)(2,1)} %get-tuple-element.37) | copy-start | bytes 3145732
  146.8 111.9 %all-to-all-start.1 = ((bf16[64,64,128]{2,1,0:T(8,128)(2,1)}), bf16[64,64,128]{2,1,0:T(8,128)(2,1)S(1)}, u32[]{:S(2)}, u32[]{:S(2)}) async-start(bf16[64,64,128]{2,1,0:T(8,128)(2,1)} %copy.139), calls=%async_computation.1 | async-start | bytes 2097152 | tf_op jit(solution)/shard_map/all_to_all | solution.py:110
  192.1 62.9 %copy-start.8 = (f32[65,16,128]{2,1,0:T(8,128)S(1)}, f32[65,16,128]{2,1,0:T(8,128)}, u32[]{:S(2)}) copy-start(f32[65,16,128]{2,1,0:T(8,128)} %reduce-scatter.5.cloned.1.call-done) | copy-start | bytes 1597444
  256.8 6.1 %copy-start.3 = (bf16[1,128,4096]{1,2,0:T(8,128)(2,1)S(1)}, bf16[1,128,4096]{1,2,0:T(8,128)(2,1)}, u32[]{:S(2)}) copy-start(bf16[1,128,4096]{1,2,0:T(8,128)(2,1)} %copy-done.2) | copy-start | bytes 3145732
  258.7 18.2 %all-to-all-start.3 = ((f32[64,16,128]{2,1,0:T(8,128)}), f32[64,16,128]{2,1,0:T(8,128)}, u32[]{:S(2)}, u32[]{:S(2)}) async-start(f32[64,16,128]{2,1,0:T(8,128)} %copy.150), calls=%async_computation.5 | async-start | bytes 1048576 | tf_op jit(solution)/shard_map/all_to_all | solution.py:123
  264.8 2.4 copy-start.7
Sparse Core Ops, SparseCore 0:
  122.8 69.2 reduce-scatter.4
  194.7 56.5 reduce-scatter.2
where the time goes:
time: 290 us; the launch traced here: 286 us
  waiting for transfers between devices  129 us (44%)
  matrix products  81.1 us (28%)
  starting transfers between devices  38.5 us (13%)
  local copies, waits for them, and re-layouts  16.9 us (6%)
  between operations  14.6 us (5%)
  other arithmetic  6.24 us (2%)
    reduce_scatter x1, waiting for transfers between devices, local(): lax.psum_scatter(cross_re, 'dp', scatter_dimension=1, tiled=True)  57.2 us
    dot_general x20, matrix products, along_rows(): jnp.einsum('kcr,rm->kcm', spectrum, matrix, precision=lax.Precision.HIGHEST)  53.5 us
    reduce_scatter x1, waiting for transfers between devices, local(): lax.psum_scatter(cross_im, 'dp', scatter_dimension=1, tiled=True)  33.2 us
    all_to_all x1, waiting for transfers between devices, local(): lax.all_to_all(blocks(signal), 'seq', split_axis=0, concat_axis=0, tiled=...  21.2 us
    all_to_all x1, starting transfers between devices, local(): lax.all_to_all(blocks(signal), 'seq', split_axis=0, concat_axis=0, tiled=...  15.7 us
    unnamed x31, local copies, waits for them, and re-layouts  13.2 us
    dot_general x3, matrix products, forward(): jnp.einsum('ka,acr->kcr', cos_first, values, precision=lax.Precision.HIGH...  13.2 us
    all_to_all x1, starting transfers between devices, local(): lax.all_to_all(corr_time.astype(jnp.bfloat16), 'seq', split_axis=0, conca...  10.8 us
  transfers between devices with their start and end apart: 6, of which 5 were waited for; matrix products, arithmetic and copies ran while one was open for 20% of the time, Pallas kernels for 0%

commit v1 on v0

v1 whole, which is shorter than its diff:
```python
import functools
import math

import jax
import jax.numpy as jnp
import ml_dtypes
import numpy as np
from jax import lax
from jax.experimental import pallas as pl
from jax.experimental.pallas import tpu as pltpu
from jax.sharding import PartitionSpec as P

MESH = pl.DeviceIdType.MESH
BF = jnp.bfloat16
F32 = jnp.float32

ROWS = 128
BLOCKS = 64
OWN = 16
SEQS = 4
ZS = 8
PLANE = 32
SIZE = 2 * ROWS * BLOCKS


def split(table):
    high = table.astype(ml_dtypes.bfloat16)
    low = (table - high.astype(np.float64)).astype(ml_dtypes.bfloat16)
    return high, low


def make_tables():
    half = np.arange(BLOCKS) + 0.5
    rows = np.arange(ROWS)
    slot = np.arange(BLOCKS)
    zh, plane = slot // PLANE, slot % PLANE
    arrived = (plane // 2) * 4 + zh * 2 + plane % 2
    out = {}
    for name, blocks in (("d", arrived), ("f", slot)):
        angle = 2 * np.pi * half[:, None] * blocks[None, :] / (2 * BLOCKS)
        first = np.concatenate([np.cos(angle), -np.sin(angle)], axis=0)
        high, low = split(first)
        out["e" + name] = np.concatenate([high, low] if name == "d" else [high, high, low], axis=1)
        high, low = split(first.T * (2.0 / SIZE))
        out["i" + name] = np.concatenate([high, low], axis=1)
    angle = 2 * np.pi * half[:, None] * rows[None, :] / SIZE
    out["wc"] = np.tile(np.cos(angle), (1, 2)).astype(np.float32)
    out["ws"] = np.tile(np.sin(angle), (1, 2)).astype(np.float32)
    angle = 2 * np.pi * rows[:, None] * rows[None, :] / ROWS
    cos, sin = np.cos(angle), np.sin(angle)
    out["dh"], out["dl"] = split(np.block([[cos, -sin], [sin, cos]]))
    out["bh"], out["bl"] = split(np.block([[cos, sin], [-sin, cos]]))
    return out


NAMES = ("ed", "ef", "id", "if", "wc", "ws", "dh", "dl", "bh", "bl")


def dot(a, b):
    return jnp.dot(a, b, preferred_element_type=F32)


def body(*refs):
    (g_h, q_h, k_h, v_h, c_h, f_h) = refs[:6]
    tables_h = refs[6 : 6 + len(NAMES)]
    gq_h, gk_h, gv_h, fg_h = refs[16:20]
    (g, q, k, v, co, filt, *tables) = refs[20 : 27 - 1 + len(NAMES)]
    ed, ef, idt, ift, wc, ws, dh, dl, bh, bl = tables
    (
        gq, gk, gv, fgo,
        zs_s, zs_p, zr_s, zr_p, pr_s, pr_p,
        gout, rp, gt,
        spec, fspec, acc, xs, zb, fgs, fgr,
        in_sem, out_sem, self_sem,
        zsend, zrecv, psend, precv, fsend, frecv,
    ) = refs[26 + len(NAMES) :]

    dp = lax.axis_index("dp")
    seq = lax.axis_index("seq")
    zh = (seq // 2) % 2
    z = zh * 4 + dp
    py, px, pc = seq // 16, (seq // 4) % 4, seq % 2
    w_me = dp * 2 + zh
    q_me = py * 8 + px * 2 + pc

    def z_peer(step):
        other = (z + step) % ZS
        return (other % 4, py * 16 + px * 4 + (other // 4) * 2 + pc), (other % 4) * 2 + other // 4

    def plane_peer(step):
        y, x, c = (py + step // 8) % 4, (px + (step // 2) % 4) % 4, (pc + step % 2) % 2
        return (dp, y * 16 + x * 4 + zh * 2 + c), y * 8 + x * 2 + c

    pairs = [(g_h.at[0], g), (q_h.at[0], q), (k_h.at[0], k), (v_h.at[0], v), (c_h.at[0], co)]
    pairs.append((f_h.at[pl.ds(dp * OWN, OWN), :], filt))
    pairs += list(zip(tables_h, tables))
    loads = [pltpu.make_async_copy(a, b, in_sem.at[n]) for n, (a, b) in enumerate(pairs)]
    for copy in loads:
        copy.start()

    barrier = pltpu.get_barrier_semaphore()

    @pl.loop(1, ZS)
    def _(step):
        pl.semaphore_signal(barrier, inc=1, device_id=z_peer(step)[0], device_id_type=MESH)

    @pl.loop(1, PLANE)
    def _(step):
        pl.semaphore_signal(barrier, inc=1, device_id=plane_peer(step)[0], device_id_type=MESH)

    def turn(left, right, out):
        @pl.loop(0, 32)
        def _(m):
            lanes = pl.ds(pl.multiple_of(m * 128, 128), 128)
            value = left[:, lanes].astype(F32) * right[:, lanes].astype(F32)
            tiles = value.T.astype(BF)
            for t in range(8):
                out[(t % 4) * 2 + m % 2, (m // 2) * 2 + t // 4] = tiles[t * OWN : (t + 1) * OWN]

    def z_start(n, src, dst):
        @pl.loop(1, ZS)
        def _(step):
            device, slot = z_peer(step)
            pltpu.make_async_remote_copy(
                src_ref=src.at[slot], dst_ref=dst.at[w_me], send_sem=zsend.at[n], recv_sem=zrecv.at[n],
                device_id=device, device_id_type=MESH,
            ).start()
        pltpu.make_async_copy(src.at[w_me], dst.at[w_me], self_sem.at[n]).start()

    def z_wait_send(n, src):
        pltpu.make_async_copy(src.at[pl.ds(0, ZS - 1)], src.at[pl.ds(0, ZS - 1)], zsend.at[n]).wait()

    def z_wait_recv(n, src, dst):
        pltpu.make_async_copy(src.at[w_me], dst.at[w_me], self_sem.at[n]).wait()
        pltpu.make_async_copy(dst.at[pl.ds(0, ZS - 1)], dst.at[pl.ds(0, ZS - 1)], zrecv.at[n]).wait()

    def plane_start(n, src, dst):
        @pl.loop(1, PLANE)
        def _(step):
            device, slot = plane_peer(step)
            pltpu.make_async_remote_copy(
                src_ref=src.at[:, slot], dst_ref=dst.at[:, q_me], send_sem=psend.at[n], recv_sem=precv.at[n],
                device_id=device, device_id_type=MESH,
            ).start()
        pltpu.make_async_copy(src.at[:, q_me], dst.at[:, q_me], self_sem.at[3 + n]).start()

    def plane_wait_send(n, src):
        part = src.at[:, pl.ds(0, PLANE - 1)]
        pltpu.make_async_copy(part, part, psend.at[n]).wait()

    def plane_wait_recv(n, src, dst):
        pltpu.make_async_copy(src.at[:, q_me], dst.at[:, q_me], self_sem.at[3 + n]).wait()
        part = dst.at[:, pl.ds(0, PLANE - 1)]
        pltpu.make_async_copy(part, part, precv.at[n]).wait()

    def channel(i):
        return xs[pl.ds(i, BLOCKS, stride=OWN), :]

    def second(rows, high, low):
        data = zb[rows, :]
        return dot(data, high[...]) + dot(data, low[...])

    def forward_first(exact):
        for pair in range(0, OWN, 2):
            x = jnp.concatenate([channel(pair), channel(pair + 1)], axis=1)
            if exact:
                x = x.astype(BF)
                y = dot(ed[...], jnp.concatenate([x, x], axis=0))
            else:
                high = x.astype(BF)
                low = (x - high.astype(F32)).astype(BF)
                y = dot(ef[...], jnp.concatenate([high, low, high], axis=0))
            re, im = y[:BLOCKS], y[BLOCKS:]
            turned_re = re * wc[...] + im * ws[...]
            turned_im = im * wc[...] - re * ws[...]
            for j in range(2):
                lanes = slice(j * ROWS, (j + 1) * ROWS)
                value = jnp.concatenate([turned_re[:, lanes], turned_im[:, lanes]], axis=1)
                zb[(pair + j) * BLOCKS : (pair + j + 1) * BLOCKS, :] = value.astype(BF)

    def inverse(chunk, table):
        inner = second(slice(chunk * 256, (chunk + 1) * 256), bh, bl)
        for pair in range(0, 4, 2):
            parts = []
            for j in (pair, pair + 1):
                re, im = inner[j * BLOCKS : (j + 1) * BLOCKS, :ROWS], inner[j * BLOCKS : (j + 1) * BLOCKS, ROWS:]
                cos, sin = wc[:, :ROWS], ws[:, :ROWS]
                parts.append(jnp.concatenate([re * cos - im * sin, im * cos + re * sin], axis=0).astype(BF))
            both = jnp.concatenate(parts, axis=1)
            y = dot(table[...], jnp.concatenate([both, both], axis=0))
            for j in range(2):
                xs[pl.ds(chunk * 4 + pair + j, BLOCKS, stride=OWN), :] = y[:, j * ROWS : (j + 1) * ROWS]

    loads[0].wait()
    loads[1].wait()
    turn(g, q, zs_s)
    pl.semaphore_wait(barrier, ZS - 1 + PLANE - 1)
    z_start(0, zs_s, zr_s)
    loads[2].wait()
    loads[3].wait()
    turn(k, v, zs_p)

    loads[4].wait()

    @pl.loop(0, 32)
    def _(m):
        lanes = pl.ds(pl.multiple_of(m * 128, 128), 128)
        gq[:, lanes] = (g[:, lanes].astype(F32) * co[:, lanes].astype(F32)).astype(BF)

    gq_out = pltpu.make_async_copy(gq, gq_h.at[0], out_sem.at[0])
    gq_out.start()

    for copy in loads[5:]:
        copy.wait()

    @pl.loop(0, BLOCKS)
    def _(a):
        rows = pl.ds(pl.multiple_of(a * OWN, OWN), OWN)
        xs[rows, :] = filt[:, pl.ds(pl.multiple_of(a * ROWS, ROWS), ROWS)]

    forward_first(False)
    for chunk in range(4):
        rows = slice(chunk * 256, (chunk + 1) * 256)
        fspec[rows, :] = second(rows, dh, dl)

    z_wait_send(0, zs_s)
    z_start(1, zs_p, zr_p)
    z_wait_recv(0, zs_s, zr_s)
    plane_start(0, zr_s, pr_s)
    plane_wait_recv(0, zr_s, pr_s)

    @pl.loop(0, SEQS)
    def _(b):
        xs[...] = pr_s[pl.ds(b * 2, 2)].astype(F32).reshape(BLOCKS * OWN, ROWS)
        forward_first(True)
        for chunk in range(4):
            rows = slice(chunk * 256, (chunk + 1) * 256)
            s = second(rows, dh, dl)
            spec[b, rows, :] = s
            s_re, s_im = s[:, :ROWS], s[:, ROWS:]
            f_re, f_im = fspec[rows, :ROWS], fspec[rows, ROWS:]
            value = jnp.concatenate([f_re * s_re + f_im * s_im, f_re * s_im - f_im * s_re], axis=1)
            zb[rows, :] = value.astype(BF)
            inverse(chunk, idt)
        gout[pl.ds(b * 2, 2)] = xs[...].astype(BF).reshape(2, PLANE, OWN, ROWS)

    plane_start(2, gout, rp)
    z_wait_recv(1, zs_p, zr_p)
    plane_start(1, zr_p, pr_p)
    plane_wait_recv(2, gout, rp)
    z_start(2, rp, gt)
    plane_wait_recv(1, zr_p, pr_p)

    @pl.loop(0, SEQS)
    def _(b):
        xs[...] = pr_p[pl.ds(b * 2, 2)].astype(F32).reshape(BLOCKS * OWN, ROWS)
        forward_first(True)
        for chunk in range(4):
            rows = slice(chunk * 256, (chunk + 1) * 256)
            p = second(rows, dh, dl)
            p_re, p_im = p[:, :ROWS], p[:, ROWS:]
            s_re, s_im = spec[b, rows, :ROWS], spec[b, rows, ROWS:]
            value = jnp.concatenate([p_re * s_re + p_im * s_im, p_re * s_im - p_im * s_re], axis=1)
            acc[rows, :] = jnp.where(b == 0, value, acc[rows, :] + value)

    zb[...] = acc[...].astype(BF)
    for chunk in range(4):
        inverse(chunk, ift)

    @pl.loop(0, BLOCKS)
    def _(a):
        rows = pl.ds(pl.multiple_of(a * OWN, OWN), OWN)
        fgs[a // 16, :, pl.ds(pl.multiple_of((a % 16) * ROWS, ROWS), ROWS)] = xs[rows, :].astype(BF)

    @pl.loop(1, SEQS)
    def _(step):
        other = (dp + step) % SEQS
        pltpu.make_async_remote_copy(
            src_ref=fgs.at[other], dst_ref=fgr.at[dp], send_sem=fsend, recv_sem=frecv,
            device_id=(other, seq), device_id_type=MESH,
        ).start()

    fgr[dp] = fgs[dp]

    z_wait_recv(2, rp, gt)

    @pl.loop(0, 32)
    def _(m):
        lanes = pl.ds(pl.multiple_of(m * 128, 128), 128)
        tiles = [gt[(t % 4) * 2 + m % 2, (m // 2) * 2 + t // 4] for t in range(8)]
        value = jnp.concatenate(tiles, axis=0).astype(F32).T
        gk[:, lanes] = (value * v[:, lanes].astype(F32)).astype(BF)
        gv[:, lanes] = (value * k[:, lanes].astype(F32)).astype(BF)

    outs = [
        pltpu.make_async_copy(gk, gk_h.at[0], out_sem.at[1]),
        pltpu.make_async_copy(gv, gv_h.at[0], out_sem.at[2]),
    ]
    for copy in outs:
        copy.start()

    pltpu.make_async_copy(fgr.at[pl.ds(0, SEQS - 1)], fgr.at[pl.ds(0, SEQS - 1)], frecv).wait()
    scale = 1.0 / math.sqrt(SEQS * ROWS * BLOCKS)
    for d in range(SEQS):
        fgo[d * OWN : (d + 1) * OWN, :] = fgr[d].astype(F32) * scale
    outs.append(pltpu.make_async_copy(fgo, fg_h, out_sem.at[3]))
    outs[-1].start()

    z_wait_send(1, zs_p)
    z_wait_send(2, rp)
    plane_wait_send(0, zr_s)
    plane_wait_send(1, zr_p)
    plane_wait_send(2, gout)
    pltpu.make_async_copy(fgs.at[pl.ds(0, SEQS - 1)], fgs.at[pl.ds(0, SEQS - 1)], fsend).wait()
    gq_out.wait()
    for copy in outs:
        copy.wait()


def local(grad_out, query_proj, key_proj, value_proj, conv_out, filters):
    tables = make_tables()
    values = [jnp.asarray(tables[name]) for name in NAMES]
    rows, channels = grad_out.shape[1:]
    wide = pltpu.VMEM((rows, channels), BF)
    moved = pltpu.VMEM((ZS, PLANE, OWN, ROWS), BF)
    any_spec = pl.BlockSpec(memory_space=pl.ANY)
    dma = pltpu.SemaphoreType.DMA
    return pl.pallas_call(
        body,
        out_shape=[jax.ShapeDtypeStruct(grad_out.shape, BF)] * 3
        + [jax.ShapeDtypeStruct((SEQS * OWN, filters.shape[1] // SEQS), F32)],
        in_specs=[any_spec] * (6 + len(NAMES)),
        out_specs=[any_spec] * 4,
        scratch_shapes=[wide] * 5
        + [pltpu.VMEM((OWN, filters.shape[1]), F32)]
        + [pltpu.VMEM(a.shape, a.dtype) for a in values]
        + [wide] * 3
        + [pltpu.VMEM((SEQS * OWN, filters.shape[1] // SEQS), F32)]
        + [moved] * 9
        + [
            pltpu.VMEM((SEQS, OWN * BLOCKS, 2 * ROWS), F32),
            pltpu.VMEM((OWN * BLOCKS, 2 * ROWS), F32),
            pltpu.VMEM((OWN * BLOCKS, 2 * ROWS), F32),
            pltpu.VMEM((OWN * BLOCKS, ROWS), F32),
            pltpu.VMEM((OWN * BLOCKS, 2 * ROWS), BF),
            pltpu.VMEM((SEQS, OWN, filters.shape[1] // SEQS), BF),
            pltpu.VMEM((SEQS, OWN, filters.shape[1] // SEQS), BF),
            dma((6 + len(NAMES),)),
            dma((4,)),
            dma((6,)),
            dma((3,)),
            dma((3,)),
            dma((3,)),
            dma((3,)),
            dma(()),
            dma(()),
        ],
        compiler_params=pltpu.CompilerParams(
            collective_id=0, has_side_effects=True, vmem_limit_bytes=56 * 1024 * 1024
        ),
    )(grad_out, query_proj, key_proj, value_proj, conv_out, filters, *values)


def solution(mesh):
    across = P("dp", "seq", None)
    return jax.shard_map(
        local,
        mesh=mesh,
        in_specs=(across,) * 5 + (P("seq", None),),
        out_specs=(across,) * 3 + (P("seq", "dp"),),
        check_vma=False,
    )
```

time: 290 us -> 115 us (0.40); the launches traced: 286 us -> 114 us
  waiting for transfers between devices: 129 us -> 0 us
  Pallas kernels: 0 us -> 108 us
  matrix products: 81.1 us -> 0 us
  starting transfers between devices: 38.5 us -> 0 us
  between operations: 14.6 us -> 0.66 us
  local copies, waits for them, and re-layouts: 16.9 us -> 5.18 us
  other arithmetic: 6.24 us -> 0 us
    pallas_call x0 -> x1, Pallas kernels: none -> 108 us  [local(): pl.pallas_call(body, out_shape=[jax.ShapeDtypeStruct(grad_out.shape, BF)]...]
    reduce_scatter x2 -> x0, waiting for transfers between devices: 90.4 us -> none  [the longest x1 57.2 us: local(): lax.psum_scatter(cross_re, 'dp', scatter_dimension=1, tiled=True)]
    dot_general x30 -> x0, matrix products: 81.1 us -> none  [the longest x20 53.5 us: along_rows(): jnp.einsum('kcr,rm->kcm', spectrum, matrix, precision=lax.Precision.HIGHEST)]
    all_to_all x4 -> x0, starting transfers between devices: 38.1 us -> none  [the longest x1 15.7 us: local(): lax.all_to_all(blocks(signal), 'seq', split_axis=0, concat_axis=0, tiled=...]
    all_to_all x4 -> x0, waiting for transfers between devices: 37.5 us -> none  [the longest x1 21.2 us: local(): lax.all_to_all(blocks(signal), 'seq', split_axis=0, concat_axis=0, tiled=...]
    unnamed x31 -> x10, local copies, waits for them, and re-layouts: 13.2 us -> 5.18 us
    convert_element_type x2 -> x0, other arithmetic: 3.1 us -> none  [the longest x1 1.79 us: local(): (grad_rows * query_proj[0].astype(jnp.float32)).astype(jnp.bfloat16)]
  transfers between devices with their start and end apart: 6 -> 0, of which waited for: 5 -> 0; matrix products, arithmetic and copies ran while one was open for 20% -> 0% of each run, Pallas kernels for 0% -> 0%
where the time goes in v1:
time: 115 us; the launch traced here: 114 us
  Pallas kernels  108 us (94%)
  local copies, waits for them, and re-layouts  5.18 us (5%)
    pallas_call x1, Pallas kernels, local(): pl.pallas_call(body, out_shape=[jax.ShapeDtypeStruct(grad_out.shape, BF)]...  108 us
    unnamed x10, local copies, waits for them, and re-layouts  5.18 us

profile of v1, /device:TPU:1, one launch (start us, length us, event | category | flops | bytes accessed | tf_op | source)
XLA Modules:
  0.0 114.1 jit_solution(8783024665273573299)
XLA Ops:
  0.6 108.2 %shard_map.183 = (bf16[1,128,4096]{2,1,0:T(8,128)(2,1)}, bf16[1,128,4096]{2,1,0:T(8,128)(2,1)}, bf16[1,128,4096]{2,1,0:T(8,128)(2,1)}, f32[64,2048]{1,0:T(8,128)}) custom-call(bf16[1,128,4096]{2,1,0:T(8,128)(2,1)} %refs_0_.1, bf16[1,128,4096]{2,1,0:T(8,128)(2,1)} %refs_1_.1, bf16[1,128,4096]{2,1,0:T(8,128)(2,1)} %refs_2_.1, bf16[1,128,4096]{2,1,0:T(8,128)(2,1)} %refs_3_.1, ...), custom_call_target="tpu_custom_call" | custom-call | tf_op jit(solution)/shard_map/pallas_call | solution.py:328
  108.9 0.0 copy-start.1
  108.9 0.0 copy-start
  108.9 2.4 %copy.24 = bf16[1,128,4096]{2,1,0:T(8,128)(2,1)} copy(bf16[1,128,4096]{2,1,0:T(8,128)(2,1)} %get-tuple-element.8) | data formatting | bytes 2097152
  111.3 0.0 copy-done.1
  111.3 0.0 copy-start.2
  111.3 1.0 copy.25
  112.3 0.0 copy-done
  112.3 1.0 copy.26
  113.3 0.0 copy-done.2
  113.3 0.8 copy.27
Async XLA Ops:
  108.9 2.5 %copy-start.1 = (bf16[1,128,4096]{2,1,0:T(8,128)(2,1)S(1)}, bf16[1,128,4096]{2,1,0:T(8,128)(2,1)}, u32[]{:S(2)}) copy-start(bf16[1,128,4096]{2,1,0:T(8,128)(2,1)} %get-tuple-element.9) | copy-start | bytes 3145732
  108.9 3.4 %copy-start = (bf16[1,128,4096]{2,1,0:T(8,128)(2,1)S(1)}, bf16[1,128,4096]{2,1,0:T(8,128)(2,1)}, u32[]{:S(2)}) copy-start(bf16[1,128,4096]{2,1,0:T(8,128)(2,1)} %get-tuple-element.10) | copy-start | bytes 3145732
  111.3 1.9 %copy-start.2 = (f32[64,2048]{1,0:T(8,128)S(1)}, f32[64,2048]{1,0:T(8,128)}, u32[]{:S(2)}) copy-start(f32[64,2048]{1,0:T(8,128)} %get-tuple-element.11) | copy-start | bytes 1572868

commit v2 on v1

v2 whole, which is shorter than its diff:
```python
import functools
import math

import jax
import jax.numpy as jnp
import ml_dtypes
import numpy as np
from jax import lax
from jax.experimental import pallas as pl
from jax.experimental.pallas import tpu as pltpu
from jax.sharding import PartitionSpec as P

MESH = pl.DeviceIdType.MESH
BF = jnp.bfloat16
F32 = jnp.float32

ROWS = 128
BLOCKS = 64
OWN = 16
SEQS = 4
ZS = 8
PLANE = 32
SIZE = 2 * ROWS * BLOCKS


def split(table):
    high = table.astype(ml_dtypes.bfloat16)
    low = (table - high.astype(np.float64)).astype(ml_dtypes.bfloat16)
    return high, low


def make_tables():
    half = np.arange(BLOCKS) + 0.5
    rows = np.arange(ROWS)
    slot = np.arange(BLOCKS)
    zh, plane = slot // PLANE, slot % PLANE
    arrived = (plane // 2) * 4 + zh * 2 + plane % 2
    out = {}
    for name, blocks in (("d", arrived), ("f", slot)):
        angle = 2 * np.pi * half[:, None] * blocks[None, :] / (2 * BLOCKS)
        first = np.concatenate([np.cos(angle), -np.sin(angle)], axis=0)
        high, low = split(first)
        out["e" + name] = np.concatenate([high, low] if name == "d" else [high, high, low], axis=1)
        high, low = split(first.T * (2.0 / SIZE))
        out["i" + name] = np.concatenate([high, high, low], axis=1)
    angle = 2 * np.pi * half[:, None] * rows[None, :] / SIZE
    out["wc"] = np.tile(np.cos(angle), (1, 2)).astype(np.float32)
    out["ws"] = np.tile(np.sin(angle), (1, 2)).astype(np.float32)
    angle = 2 * np.pi * rows[:, None] * rows[None, :] / ROWS
    cos, sin = np.cos(angle), np.sin(angle)
    out["dh"], out["dl"] = split(np.block([[cos, -sin], [sin, cos]]))
    out["bh"], out["bl"] = split(np.block([[cos, sin], [-sin, cos]]))
    return out


NAMES = ("ed", "ef", "id", "if", "wc", "ws", "dh", "dl", "bh", "bl")


def dot(a, b):
    return jnp.dot(a, b, preferred_element_type=F32)


def parts(value):
    high = value.astype(BF)
    return high, (value - high.astype(F32)).astype(BF)


def body(*refs):
    (g_h, q_h, k_h, v_h, f_h) = refs[:5]
    tables_h = refs[5 : 5 + len(NAMES)]
    gt, fgr = refs[15:17]
    (g, q, k, v, filt, *tables) = refs[17 : 22 + len(NAMES)]
    ed, ef, idt, ift, wc, ws, dh, dl, bh, bl = tables
    (
        sent_s, sent_p, got_s, got_p, gout,
        spec, fspec, acc, xs, zh_b, zl_b, fgs,
        in_sem, self_sem, gate, send, recv, fsend, frecv,
    ) = refs[22 + len(NAMES) :]

    dp = lax.axis_index("dp")
    seq = lax.axis_index("seq")
    z = (seq // 2) % 2 * 4 + dp
    py, px, pc = seq // 16, (seq // 4) % 4, seq % 2

    column = []
    for step in range(ZS):
        other = (z + step) % ZS
        column.append((other % 4, (other // 4) * 2, ((other % 4) * 2 + other // 4) * PLANE))
    me = column[0][2] + py * 8 + px * 2 + pc

    def in_plane(step):
        y, x, c = (py + step // 8) % 4, (px + (step // 2) % 4) % 4, (pc + step % 2) % 2
        return y * 16 + x * 4 + c, y * 8 + x * 2 + c

    pairs = [(g_h.at[0], g), (q_h.at[0], q), (k_h.at[0], k), (v_h.at[0], v)]
    pairs.append((f_h.at[pl.ds(dp * OWN, OWN), :], filt))
    pairs += list(zip(tables_h, tables))
    loads = [pltpu.make_async_copy(a, b, in_sem.at[n]) for n, (a, b) in enumerate(pairs)]
    for copy in loads:
        copy.start()

    barrier = pltpu.get_barrier_semaphore()
    for dpi, add, _ in column[1:]:
        device = (dpi, py * 16 + px * 4 + pc + add)
        pl.semaphore_signal(barrier, inc=1, device_id=device, device_id_type=MESH)

    @pl.loop(1, PLANE)
    def _(step):
        device = (dp, in_plane(step)[0] + column[0][1])
        pl.semaphore_signal(barrier, inc=1, device_id=device, device_id_type=MESH)

    def turn(left, right, out):
        @pl.loop(0, 32)
        def _(m):
            lanes = pl.ds(pl.multiple_of(m * 128, 128), 128)
            value = left[:, lanes].astype(F32) * right[:, lanes].astype(F32)
            tiles = value.T.astype(BF)
            for t in range(8):
                out[((t % 4) * 2 + m % 2) * PLANE + (m // 2) * 2 + t // 4] = tiles[t * OWN : (t + 1) * OWN]

    def exchange(n, src, dst):
        def one(entry, base, slot):
            pltpu.make_async_remote_copy(
                src_ref=src.at[entry[2] + slot], dst_ref=dst.at[me], send_sem=send.at[n], recv_sem=recv.at[n],
                device_id=(entry[0], base + entry[1]), device_id_type=MESH,
            ).start()

        base, slot = in_plane(0)
        for entry in column[1:]:
            one(entry, base, slot)
        pltpu.make_async_copy(src.at[me], dst.at[me], self_sem.at[n]).start()

        @pl.loop(1, PLANE)
        def _(step):
            base, slot = in_plane(step)
            for entry in column:
                one(entry, base, slot)

    def sent(n, src):
        part = src.at[pl.ds(0, ZS * PLANE - 1)]
        pltpu.make_async_copy(part, part, send.at[n]).wait()

    def arrived(n, src, dst):
        pltpu.make_async_copy(src.at[me], dst.at[me], self_sem.at[n]).wait()
        part = dst.at[pl.ds(0, ZS * PLANE - 1)]
        pltpu.make_async_copy(part, part, recv.at[n]).wait()

    def channel(i):
        return xs[pl.ds(i, BLOCKS, stride=OWN), :]

    def store(rows, value):
        zh_b[rows, :], zl_b[rows, :] = parts(value)

    def second(rows, high, low):
        return dot(zh_b[rows, :], high[...]) + dot(zl_b[rows, :], high[...]) + dot(zh_b[rows, :], low[...])

    def forward_first(exact):
        for pair in range(0, OWN, 2):
            x = jnp.concatenate([channel(pair), channel(pair + 1)], axis=1)
            if exact:
                x = x.astype(BF)
                y = dot(ed[...], jnp.concatenate([x, x], axis=0))
            else:
                high, low = parts(x)
                y = dot(ef[...], jnp.concatenate([high, low, high], axis=0))
            re, im = y[:BLOCKS], y[BLOCKS:]
            turned_re = re * wc[...] + im * ws[...]
            turned_im = im * wc[...] - re * ws[...]
            for j in range(2):
                lanes = slice(j * ROWS, (j + 1) * ROWS)
                value = jnp.concatenate([turned_re[:, lanes], turned_im[:, lanes]], axis=1)
                store(slice((pair + j) * BLOCKS, (pair + j + 1) * BLOCKS), value)

    def inverse(chunk, table):
        inner = second(slice(chunk * 256, (chunk + 1) * 256), bh, bl)
        for pair in range(0, 4, 2):
            both = []
            for j in (pair, pair + 1):
                re, im = inner[j * BLOCKS : (j + 1) * BLOCKS, :ROWS], inner[j * BLOCKS : (j + 1) * BLOCKS, ROWS:]
                cos, sin = wc[:, :ROWS], ws[:, :ROWS]
                both.append(jnp.concatenate([re * cos - im * sin, im * cos + re * sin], axis=0))
            high, low = parts(jnp.concatenate(both, axis=1))
            y = dot(table[...], jnp.concatenate([high, low, high], axis=0))
            for j in range(2):
                xs[pl.ds(chunk * 4 + pair + j, BLOCKS, stride=OWN), :] = y[:, j * ROWS : (j + 1) * ROWS]

    loads[0].wait()
    loads[1].wait()
    turn(g, q, sent_s)
    pl.semaphore_wait(barrier, ZS - 1 + PLANE - 1)
    for dpi, add, _ in column[1:]:
        device = (dpi, py * 16 + px * 4 + pc + add)
        pl.semaphore_signal(gate, inc=1, device_id=device, device_id_type=MESH)
    pl.semaphore_wait(gate, ZS - 1)
    exchange(0, sent_s, got_s)
    loads[2].wait()
    loads[3].wait()
    turn(k, v, sent_p)

    for copy in loads[4:]:
        copy.wait()

    @pl.loop(0, BLOCKS)
    def _(a):
        rows = pl.ds(pl.multiple_of(a * OWN, OWN), OWN)
        xs[rows, :] = filt[:, pl.ds(pl.multiple_of(a * ROWS, ROWS), ROWS)]

    forward_first(False)
    for chunk in range(4):
        rows = slice(chunk * 256, (chunk + 1) * 256)
        fspec[rows, :] = second(rows, dh, dl)

    sent(0, sent_s)
    exchange(1, sent_p, got_p)
    arrived(0, sent_s, got_s)

    @pl.loop(0, SEQS)
    def _(b):
        tiles = pl.ds(b * BLOCKS, BLOCKS)
        xs[...] = got_s[tiles].astype(F32).reshape(BLOCKS * OWN, ROWS)
        forward_first(True)
        for chunk in range(4):
            rows = slice(chunk * 256, (chunk + 1) * 256)
            s = second(rows, dh, dl)
            spec[b, rows, :] = s
            s_re, s_im = s[:, :ROWS], s[:, ROWS:]
            f_re, f_im = fspec[rows, :ROWS], fspec[rows, ROWS:]
            store(rows, jnp.concatenate([f_re * s_re + f_im * s_im, f_re * s_im - f_im * s_re], axis=1))
            inverse(chunk, idt)
        gout[tiles] = xs[...].astype(BF).reshape(BLOCKS, OWN, ROWS)

    exchange(2, gout, gt)
    arrived(1, sent_p, got_p)

    @pl.loop(0, SEQS)
    def _(b):
        xs[...] = got_p[pl.ds(b * BLOCKS, BLOCKS)].astype(F32).reshape(BLOCKS * OWN, ROWS)
        forward_first(True)
        for chunk in range(4):
            rows = slice(chunk * 256, (chunk + 1) * 256)
            p = second(rows, dh, dl)
            p_re, p_im = p[:, :ROWS], p[:, ROWS:]
            s_re, s_im = spec[b, rows, :ROWS], spec[b, rows, ROWS:]
            value = jnp.concatenate([p_re * s_re + p_im * s_im, p_re * s_im - p_im * s_re], axis=1)
            acc[rows, :] = jnp.where(b == 0, value, acc[rows, :] + value)

    for chunk in range(4):
        rows = slice(chunk * 256, (chunk + 1) * 256)
        store(rows, acc[rows, :])
        inverse(chunk, ift)

    @pl.loop(0, BLOCKS)
    def _(a):
        rows = pl.ds(pl.multiple_of(a * OWN, OWN), OWN)
        fgs[a // 16, :, pl.ds(pl.multiple_of((a % 16) * ROWS, ROWS), ROWS)] = xs[rows, :].astype(BF)

    for step in range(1, SEQS):
        other = (dp + step) % SEQS
        pltpu.make_async_remote_copy(
            src_ref=fgs.at[other], dst_ref=fgr.at[dp], send_sem=fsend, recv_sem=frecv,
            device_id=(other, seq), device_id_type=MESH,
        ).start()
    own = pltpu.make_async_copy(fgs.at[dp], fgr.at[dp], self_sem.at[3])
    own.start()

    sent(1, sent_p)
    sent(2, gout)
    arrived(2, gout, gt)
    own.wait()
    pltpu.make_async_copy(fgr.at[pl.ds(0, SEQS - 1)], fgr.at[pl.ds(0, SEQS - 1)], frecv).wait()
    pltpu.make_async_copy(fgs.at[pl.ds(0, SEQS - 1)], fgs.at[pl.ds(0, SEQS - 1)], fsend).wait()


def finish(g, k, v, co, gt, fgr, gq, gk, gv, fg):
    gq[0] = (g[0].astype(F32) * co[0].astype(F32)).astype(BF)
    for m in range(gt.shape[2] * 2):
        lanes = slice(m * 128, (m + 1) * 128)
        tiles = [gt[t % 4, m % 2, m // 2, t // 4] for t in range(8)]
        value = jnp.concatenate(tiles, axis=0).astype(F32).T
        gk[0, :, lanes] = (value * v[0, :, lanes].astype(F32)).astype(BF)
        gv[0, :, lanes] = (value * k[0, :, lanes].astype(F32)).astype(BF)
    fg[...] = fgr[...].astype(F32).reshape(fg.shape) * (1.0 / math.sqrt(SEQS * ROWS * BLOCKS))


def local(grad_out, query_proj, key_proj, value_proj, conv_out, filters):
    tables = make_tables()
    values = [jnp.asarray(tables[name]) for name in NAMES]
    rows, channels = grad_out.shape[1:]
    taps = filters.shape[1] // SEQS
    wide = pltpu.VMEM((rows, channels), BF)
    moved = pltpu.VMEM((ZS * PLANE, OWN, ROWS), BF)
    any_spec = pl.BlockSpec(memory_space=pl.ANY)
    dma = pltpu.SemaphoreType.DMA
    gt, fgr = pl.pallas_call(
        body,
        out_shape=[
            jax.ShapeDtypeStruct((ZS * PLANE, OWN, ROWS), BF),
            jax.ShapeDtypeStruct((SEQS, OWN, taps), BF),
        ],
        in_specs=[any_spec] * (5 + len(NAMES)),
        out_specs=[any_spec] * 2,
        scratch_shapes=[wide] * 4
        + [pltpu.VMEM((OWN, filters.shape[1]), F32)]
        + [pltpu.VMEM(a.shape, a.dtype) for a in values]
        + [moved] * 5
        + [
            pltpu.VMEM((SEQS, OWN * BLOCKS, 2 * ROWS), F32),
            pltpu.VMEM((OWN * BLOCKS, 2 * ROWS), F32),
            pltpu.VMEM((OWN * BLOCKS, 2 * ROWS), F32),
            pltpu.VMEM((OWN * BLOCKS, ROWS), F32),
            pltpu.VMEM((OWN * BLOCKS, 2 * ROWS), BF),
            pltpu.VMEM((OWN * BLOCKS, 2 * ROWS), BF),
            pltpu.VMEM((SEQS, OWN, taps), BF),
            dma((5 + len(NAMES),)),
            dma((4,)),
            pltpu.SemaphoreType.REGULAR,
            dma((3,)),
            dma((3,)),
            dma(()),
            dma(()),
        ],
        compiler_params=pltpu.CompilerParams(
            collective_id=0, has_side_effects=True, vmem_limit_bytes=56 * 1024 * 1024
        ),
    )(grad_out, query_proj, key_proj, value_proj, filters, *values)

    steps = 4
    block = pl.BlockSpec((1, rows, channels // steps), lambda i: (0, 0, i))
    return pl.pallas_call(
        finish,
        grid=(steps,),
        out_shape=[jax.ShapeDtypeStruct(grad_out.shape, BF)] * 3
        + [jax.ShapeDtypeStruct((SEQS * OWN, taps), F32)],
        in_specs=[block] * 4
        + [
            pl.BlockSpec((4, 2, 16 // steps, 2, OWN, ROWS), lambda i: (0, 0, i, 0, 0, 0)),
            pl.BlockSpec((SEQS, OWN, taps // steps), lambda i: (0, 0, i)),
        ],
        out_specs=[block] * 3 + [pl.BlockSpec((SEQS * OWN, taps // steps), lambda i: (0, i))],
        compiler_params=pltpu.CompilerParams(vmem_limit_bytes=32 * 1024 * 1024),
    )(grad_out, key_proj, value_proj, conv_out, gt.reshape(4, 2, 16, 2, OWN, ROWS), fgr)


def solution(mesh):
    across = P("dp", "seq", None)
    return jax.shard_map(
        local,
        mesh=mesh,
        in_specs=(across,) * 5 + (P("seq", None),),
        out_specs=(across,) * 3 + (P("seq", "dp"),),
        check_vma=False,
    )
```

time: 115 us -> 94 us (0.82)
  Pallas kernels: 108 us -> 90.8 us
  local copies, waits for them, and re-layouts: 5.18 us -> 2.18 us
    pallas_call x1 -> x2, Pallas kernels: 108 us -> 90.8 us  [the longest x1 87.9 us: local(): pl.pallas_call(body, out_shape=[jax.ShapeDtypeStruct((ZS * PLANE, OWN, RO...]
    unnamed x10 -> x12, local copies, waits for them, and re-layouts: 5.18 us -> 2.18 us
where the time goes in v2:
time: 94 us; the launch traced here: 93.7 us
  Pallas kernels  90.8 us (97%)
  local copies, waits for them, and re-layouts  2.18 us (2%)
    pallas_call x1, Pallas kernels, local(): pl.pallas_call(body, out_shape=[jax.ShapeDtypeStruct((ZS * PLANE, OWN, RO...  87.9 us
    pallas_call x1, Pallas kernels, local(): pl.pallas_call(finish, grid=(steps,), out_shape=[jax.ShapeDtypeStruct(gra...  2.87 us
    unnamed x12, local copies, waits for them, and re-layouts  2.18 us

profile of v2, /device:TPU:1, one launch (start us, length us, event | category | flops | bytes accessed | tf_op | source)
XLA Modules:
  0.0 93.7 jit_solution(8717712609074402595)
XLA Ops:
  0.6 0.0 copy-start.2
  0.6 0.0 copy-start.1
  0.7 0.0 copy-start
  0.7 0.0 copy-start.3
  0.7 87.9 %shard_map.183 = (bf16[256,16,128]{2,1,0:T(8,128)(2,1)}, bf16[4,16,2048]{2,1,0:T(8,128)(2,1)}) custom-call(bf16[1,128,4096]{2,1,0:T(8,128)(2,1)} %g.1, bf16[1,128,4096]{2,1,0:T(8,128)(2,1)} %refs_1_.1, bf16[1,128,4096]{2,1,0:T(8,128)(2,1)} %k.1, bf16[1,128,4096]{2,1,0:T(8,128)(2,1)} %v.1, f32[64,8192]{1,0:T(8,128)} %refs_4_.1, ...), custom_call_target="tpu_custom_call" | custom-call | tf_op jit(solution)/shard_map/pallas_call | solution.py:294
  88.6 0.0 copy-done.2
  88.6 0.0 copy-done.1
  88.6 0.0 copy-done
  88.6 0.0 copy-done.3
  88.6 0.0 copy-start.4
  88.7 1.2 %copy-done.4 = bf16[256,16,128]{2,1,0:T(8,128)(2,1)S(1)} copy-done((bf16[256,16,128]{2,1,0:T(8,128)(2,1)S(1)}, bf16[256,16,128]{2,1,0:T(8,128)(2,1)}, u32[]{:S(2)}) %copy-start.4) | copy-done | bytes 1048600
  89.9 0.0 copy-start.5
  89.9 0.9 %copy-done.5 = bf16[4,16,2048]{2,1,0:T(8,128)(2,1)S(1)} copy-done((bf16[4,16,2048]{2,1,0:T(8,128)(2,1)S(1)}, bf16[4,16,2048]{2,1,0:T(8,128)(2,1)}, u32[]{:S(2)}) %copy-start.5) | copy-done | bytes 262168
  90.8 2.9 %shard_map.184 = (bf16[1,128,4096]{2,1,0:T(8,128)(2,1)}, bf16[1,128,4096]{2,1,0:T(8,128)(2,1)}, bf16[1,128,4096]{2,1,0:T(8,128)(2,1)}, f32[64,2048]{1,0:T(8,128)}) custom-call(bf16[1,128,4096]{2,1,0:T(8,128)(2,1)S(1)} %copy-done, bf16[1,128,4096]{2,1,0:T(8,128)(2,1)S(1)} %copy-done.1, bf16[1,128,4096]{2,1,0:T(8,128)(2,1)S(1)} %copy-done.2, ...), custom_call_target="tpu_custom_call" | custom-call | tf_op jit(solution)/shard_map/pallas_call | solution.py:329
Async XLA Ops:
  0.6 88.0 %copy-start.2 = (bf16[1,128,4096]{2,1,0:T(8,128)(2,1)S(1)}, bf16[1,128,4096]{2,1,0:T(8,128)(2,1)}, u32[]{:S(2)}) copy-start(bf16[1,128,4096]{2,1,0:T(8,128)(2,1)} %v.1) | copy-start | bytes 3145732
  0.6 88.0 %copy-start.1 = (bf16[1,128,4096]{2,1,0:T(8,128)(2,1)S(1)}, bf16[1,128,4096]{2,1,0:T(8,128)(2,1)}, u32[]{:S(2)}) copy-start(bf16[1,128,4096]{2,1,0:T(8,128)(2,1)} %k.1) | copy-start | bytes 3145732
  0.7 88.0 %copy-start = (bf16[1,128,4096]{2,1,0:T(8,128)(2,1)S(1)}, bf16[1,128,4096]{2,1,0:T(8,128)(2,1)}, u32[]{:S(2)}) copy-start(bf16[1,128,4096]{2,1,0:T(8,128)(2,1)} %g.1) | copy-start | bytes 3145732
  0.7 88.0 %copy-start.3 = (bf16[1,128,4096]{2,1,0:T(8,128)(2,1)S(1)}, bf16[1,128,4096]{2,1,0:T(8,128)(2,1)}, u32[]{:S(2)}) copy-start(bf16[1,128,4096]{2,1,0:T(8,128)(2,1)} %co.1) | copy-start | bytes 3145732
  88.6 1.2 %copy-start.4 = (bf16[256,16,128]{2,1,0:T(8,128)(2,1)S(1)}, bf16[256,16,128]{2,1,0:T(8,128)(2,1)}, u32[]{:S(2)}) copy-start(bf16[256,16,128]{2,1,0:T(8,128)(2,1)} %get-tuple-element.6) | copy-start | bytes 3145732
  89.9 0.9 %copy-start.5 = (bf16[4,16,2048]{2,1,0:T(8,128)(2,1)S(1)}, bf16[4,16,2048]{2,1,0:T(8,128)(2,1)}, u32[]{:S(2)}) copy-start(bf16[4,16,2048]{2,1,0:T(8,128)(2,1)} %get-tuple-element.7.fgr) | copy-start | bytes 786436

commit v3 on v2

--- a/solution.py
+++ b/solution.py
@@ -66,16 +66,16 @@
 
 
 def body(*refs):
-    (g_h, q_h, k_h, v_h, f_h) = refs[:5]
-    tables_h = refs[5 : 5 + len(NAMES)]
-    gt, fgr = refs[15:17]
-    (g, q, k, v, filt, *tables) = refs[17 : 22 + len(NAMES)]
+    (g_h, q_h, k_h, v_h, c_h, f_h) = refs[:6]
+    tables_h = refs[6 : 6 + len(NAMES)]
+    gq, gk, gv, fg = refs[16:20]
+    (g, q, k, v, co, filt, *tables) = refs[20 : 26 + len(NAMES)]
     ed, ef, idt, ift, wc, ws, dh, dl, bh, bl = tables
     (
-        sent_s, sent_p, got_s, got_p, gout,
-        spec, fspec, acc, xs, zh_b, zl_b, fgs,
-        in_sem, self_sem, gate, send, recv, fsend, frecv,
-    ) = refs[22 + len(NAMES) :]
+        sent_s, sent_p, got_s, got_p, gout, gt, mid,
+        spec, fspec, acc, xs, zh_b, zl_b, fgs, fgr,
+        first_sem, in_sem, self_sem, gate, send, recv, back, fsend, frecv, msend, mrecv, hsend, hrecv,
+    ) = refs[26 + len(NAMES) :]
 
     dp = lax.axis_index("dp")
     seq = lax.axis_index("seq")
@@ -92,57 +92,62 @@
         y, x, c = (py + step // 8) % 4, (px + (step // 2) % 4) % 4, (pc + step % 2) % 2
         return y * 16 + x * 4 + c, y * 8 + x * 2 + c
 
-    pairs = [(g_h.at[0], g), (q_h.at[0], q), (k_h.at[0], k), (v_h.at[0], v)]
+    first = []
+    for part in range(4):
+        lanes = pl.ds(pl.multiple_of((py + part) % 4 * 1024, 1024), 1024)
+        for n, (a, b) in enumerate(((g_h, g), (q_h, q))):
+            first.append(pltpu.make_async_copy(a.at[0, :, lanes], b.at[:, lanes], first_sem.at[part * 2 + n]))
+    for copy in first:
+        copy.start()
+
+    barrier = pltpu.get_barrier_semaphore()
+    for dpi, add, _ in column[1:]:
+        device = (dpi, py * 16 + px * 4 + pc + add)
+        pl.semaphore_signal(barrier, inc=1, device_id=device, device_id_type=MESH)
+
+    @pl.loop(1, PLANE)
+    def _(step):
+        device = (dp, in_plane(step)[0] + column[0][1])
+        pl.semaphore_signal(barrier, inc=1, device_id=device, device_id_type=MESH)
+
+    pairs = [(k_h.at[0], k), (v_h.at[0], v), (c_h.at[0], co)]
     pairs.append((f_h.at[pl.ds(dp * OWN, OWN), :], filt))
     pairs += list(zip(tables_h, tables))
     loads = [pltpu.make_async_copy(a, b, in_sem.at[n]) for n, (a, b) in enumerate(pairs)]
     for copy in loads:
         copy.start()
 
-    barrier = pltpu.get_barrier_semaphore()
-    for dpi, add, _ in column[1:]:
-        device = (dpi, py * 16 + px * 4 + pc + add)
-        pl.semaphore_signal(barrier, inc=1, device_id=device, device_id_type=MESH)
-
-    @pl.loop(1, PLANE)
-    def _(step):
-        device = (dp, in_plane(step)[0] + column[0][1])
-        pl.semaphore_signal(barrier, inc=1, device_id=device, device_id_type=MESH)
-
-    def turn(left, right, out):
-        @pl.loop(0, 32)
-        def _(m):
-            lanes = pl.ds(pl.multiple_of(m * 128, 128), 128)
-            value = left[:, lanes].astype(F32) * right[:, lanes].astype(F32)
-            tiles = value.T.astype(BF)
-            for t in range(8):
-                out[((t % 4) * 2 + m % 2) * PLANE + (m // 2) * 2 + t // 4] = tiles[t * OWN : (t + 1) * OWN]
-
-    def exchange(n, src, dst):
-        def one(entry, base, slot):
-            pltpu.make_async_remote_copy(
-                src_ref=src.at[entry[2] + slot], dst_ref=dst.at[me], send_sem=send.at[n], recv_sem=recv.at[n],
-                device_id=(entry[0], base + entry[1]), device_id_type=MESH,
-            ).start()
-
-        base, slot = in_plane(0)
+    def turn(left, right, out, m):
+        lanes = pl.ds(pl.multiple_of(m * 128, 128), 128)
+        value = left[:, lanes].astype(F32) * right[:, lanes].astype(F32)
+        tiles = value.T.astype(BF)
+        for t in range(8):
+            out[((t % 4) * 2 + m % 2) * PLANE + (m // 2) * 2 + t // 4] = tiles[t * OWN : (t + 1) * OWN]
+
+    def tile(src, dst, send_sem, recv_sem, entry, place):
+        base, slot = place
+        pltpu.make_async_remote_copy(
+            src_ref=src.at[entry[2] + slot], dst_ref=dst.at[me], send_sem=send_sem, recv_sem=recv_sem,
+            device_id=(entry[0], base + entry[1]), device_id_type=MESH,
+        ).start()
+
+    def exchange(n, src, dst, recv_sem):
         for entry in column[1:]:
-            one(entry, base, slot)
+            tile(src, dst, send.at[n], recv_sem(0), entry, in_plane(0))
         pltpu.make_async_copy(src.at[me], dst.at[me], self_sem.at[n]).start()
 
         @pl.loop(1, PLANE)
         def _(step):
-            base, slot = in_plane(step)
+            place = in_plane(step)
             for entry in column:
-                one(entry, base, slot)
-
-    def sent(n, src):
-        part = src.at[pl.ds(0, ZS * PLANE - 1)]
+                tile(src, dst, send.at[n], recv_sem(step), entry, place)
+
+    def sent(n, src, count=ZS * PLANE - 1):
+        part = src.at[pl.ds(0, count)]
         pltpu.make_async_copy(part, part, send.at[n]).wait()
 
-    def arrived(n, src, dst):
-        pltpu.make_async_copy(src.at[me], dst.at[me], self_sem.at[n]).wait()
-        part = dst.at[pl.ds(0, ZS * PLANE - 1)]
+    def arrived(n, dst, count):
+        part = dst.at[pl.ds(0, count)]
         pltpu.make_async_copy(part, part, recv.at[n]).wait()
 
     def channel(i):
@@ -184,20 +189,65 @@
             for j in range(2):
                 xs[pl.ds(chunk * 4 + pair + j, BLOCKS, stride=OWN), :] = y[:, j * ROWS : (j + 1) * ROWS]
 
-    loads[0].wait()
-    loads[1].wait()
-    turn(g, q, sent_s)
+    def turn_signal(part):
+        first[2 * part].wait()
+        first[2 * part + 1].wait()
+
+        @pl.loop(0, 8)
+        def _(i):
+            turn(g, q, sent_s, (py + part) % 4 * 8 + i)
+
+    def signal_tiles(begin, end):
+        @pl.loop(begin, end)
+        def _(step):
+            place = in_plane(step)
+            for entry in column:
+                tile(sent_s, got_s, send.at[0], recv.at[0], entry, place)
+
+    turn_signal(0)
     pl.semaphore_wait(barrier, ZS - 1 + PLANE - 1)
     for dpi, add, _ in column[1:]:
         device = (dpi, py * 16 + px * 4 + pc + add)
         pl.semaphore_signal(gate, inc=1, device_id=device, device_id_type=MESH)
+    row = py * 8
+    q_me = row + px * 2 + pc
+    mine = pl.ds(column[0][2] // 4, 8)
+    for dpi, add, slot in column[1:]:
+        pltpu.make_async_remote_copy(
+            src_ref=sent_s.at[pl.ds(slot + row, 8)], dst_ref=mid.at[mine], send_sem=msend, recv_sem=mrecv,
+            device_id=(dpi, py * 16 + px * 4 + pc + add), device_id_type=MESH,
+        ).start()
+    own_mid = pltpu.make_async_copy(sent_s.at[pl.ds(column[0][2] + row, 8)], mid.at[mine], self_sem.at[0])
+    own_mid.start()
+    for part in range(1, 4):
+        turn_signal(part)
+    loads[0].wait()
+    loads[1].wait()
+
+    @pl.loop(0, 32)
+    def _(m):
+        turn(k, v, sent_p, m)
+
     pl.semaphore_wait(gate, ZS - 1)
-    exchange(0, sent_s, got_s)
-    loads[2].wait()
-    loads[3].wait()
-    turn(k, v, sent_p)
-
-    for copy in loads[4:]:
+    signal_tiles(8, 20)
+    own_mid.wait()
+    pltpu.make_async_copy(mid.at[pl.ds(0, 56)], mid.at[pl.ds(0, 56)], mrecv).wait()
+    by_source = mid.reshape(ZS, 8, OWN, ROWS)
+    got_by_source = got_s.reshape(ZS, PLANE, OWN, ROWS)
+
+    @pl.loop(1, 8)
+    def _(step):
+        base, slot = in_plane(step)
+        pltpu.make_async_remote_copy(
+            src_ref=by_source.at[:, slot - row], dst_ref=got_by_source.at[:, q_me], send_sem=hsend, recv_sem=hrecv,
+            device_id=(dp, base + column[0][1]), device_id_type=MESH,
+        ).start()
+
+    own_row = pltpu.make_async_copy(by_source.at[:, px * 2 + pc], got_by_source.at[:, q_me], self_sem.at[4])
+    own_row.start()
+    signal_tiles(20, PLANE)
+
+    for copy in loads[2:]:
         copy.wait()
 
     @pl.loop(0, BLOCKS)
@@ -210,9 +260,17 @@
         rows = slice(chunk * 256, (chunk + 1) * 256)
         fspec[rows, :] = second(rows, dh, dl)
 
-    sent(0, sent_s)
-    exchange(1, sent_p, got_p)
-    arrived(0, sent_s, got_s)
+    sent(0, sent_s, 192)
+    exchange(1, sent_p, got_p, lambda step: recv.at[1])
+
+    @pl.loop(0, 32)
+    def _(m):
+        lanes = pl.ds(pl.multiple_of(m * 128, 128), 128)
+        gq[0, :, lanes] = (g[:, lanes].astype(F32) * co[:, lanes].astype(F32)).astype(BF)
+
+    own_row.wait()
+    arrived(0, got_s, 192)
+    pltpu.make_async_copy(got_s.at[pl.ds(0, 56)], got_s.at[pl.ds(0, 56)], hrecv).wait()
 
     @pl.loop(0, SEQS)
     def _(b):
@@ -229,8 +287,9 @@
             inverse(chunk, idt)
         gout[tiles] = xs[...].astype(BF).reshape(BLOCKS, OWN, ROWS)
 
-    exchange(2, gout, gt)
-    arrived(1, sent_p, got_p)
+    exchange(2, gout, gt, lambda step: back.at[step // 8])
+    pltpu.make_async_copy(sent_p.at[me], got_p.at[me], self_sem.at[1]).wait()
+    arrived(1, got_p, ZS * PLANE - 1)
 
     @pl.loop(0, SEQS)
     def _(b):
@@ -265,21 +324,36 @@
 
     sent(1, sent_p)
     sent(2, gout)
-    arrived(2, gout, gt)
+    pltpu.make_async_copy(sent_s.at[pl.ds(0, 56)], sent_s.at[pl.ds(0, 56)], msend).wait()
+    pltpu.make_async_copy(mid.at[pl.ds(0, 56)], mid.at[pl.ds(0, 56)], hsend).wait()
+
+    pltpu.make_async_copy(gout.at[me], gt.at[me], self_sem.at[2]).wait()
+    for part in range(4):
+        count = ZS * 8 - (part == 0)
+        pltpu.make_async_copy(gt.at[pl.ds(0, count)], gt.at[pl.ds(0, count)], back.at[part]).wait()
+
+        @pl.loop(0, 8)
+        def _(i):
+            m = (py + 4 - part) % 4 * 8 + i
+            lanes = pl.ds(pl.multiple_of(m * 128, 128), 128)
+            tiles = [gt[((t % 4) * 2 + m % 2) * PLANE + (m // 2) * 2 + t // 4] for t in range(8)]
+            value = jnp.concatenate(tiles, axis=0).astype(F32).T
+            gk[0, :, lanes] = (value * v[:, lanes].astype(F32)).astype(BF)
+            gv[0, :, lanes] = (value * k[:, lanes].astype(F32)).astype(BF)
+
     own.wait()
     pltpu.make_async_copy(fgr.at[pl.ds(0, SEQS - 1)], fgr.at[pl.ds(0, SEQS - 1)], frecv).wait()
     pltpu.make_async_copy(fgs.at[pl.ds(0, SEQS - 1)], fgs.at[pl.ds(0, SEQS - 1)], fsend).wait()
-
-
-def finish(g, k, v, co, gt, fgr, gq, gk, gv, fg):
-    gq[0] = (g[0].astype(F32) * co[0].astype(F32)).astype(BF)
-    for m in range(gt.shape[2] * 2):
-        lanes = slice(m * 128, (m + 1) * 128)
-        tiles = [gt[t % 4, m % 2, m // 2, t // 4] for t in range(8)]
-        value = jnp.concatenate(tiles, axis=0).astype(F32).T
-        gk[0, :, lanes] = (value * v[0, :, lanes].astype(F32)).astype(BF)
-        gv[0, :, lanes] = (value * k[0, :, lanes].astype(F32)).astype(BF)
-    fg[...] = fgr[...].astype(F32).reshape(fg.shape) * (1.0 / math.sqrt(SEQS * ROWS * BLOCKS))
+    for d in range(SEQS):
+        fg[d * OWN : (d + 1) * OWN, :] = fgr[d].astype(F32) * (1.0 / math.sqrt(SEQS * ROWS * BLOCKS))
+
+
+def copy_out(*refs):
+    copies = [pltpu.make_async_copy(refs[n], refs[4 + n], refs[8].at[n]) for n in range(4)]
+    for copy in copies:
+        copy.start()
+    for copy in copies:
+        copy.wait()
 
 
 def local(grad_out, query_proj, key_proj, value_proj, conv_out, filters):
@@ -291,18 +365,17 @@
     moved = pltpu.VMEM((ZS * PLANE, OWN, ROWS), BF)
     any_spec = pl.BlockSpec(memory_space=pl.ANY)
     dma = pltpu.SemaphoreType.DMA
-    gt, fgr = pl.pallas_call(
+    arrays = (grad_out, query_proj, key_proj, value_proj, conv_out, filters, *values)
+    held = pl.pallas_call(
         body,
-        out_shape=[
-            jax.ShapeDtypeStruct((ZS * PLANE, OWN, ROWS), BF),
-            jax.ShapeDtypeStruct((SEQS, OWN, taps), BF),
-        ],
-        in_specs=[any_spec] * (5 + len(NAMES)),
-        out_specs=[any_spec] * 2,
-        scratch_shapes=[wide] * 4
+        out_shape=[pltpu.VMEM(grad_out.shape, BF)] * 3 + [pltpu.VMEM((SEQS * OWN, taps), F32)],
+        in_specs=[any_spec] * (6 + len(NAMES)),
+        out_specs=[pl.BlockSpec(memory_space=pltpu.VMEM)] * 4,
+        scratch_shapes=[wide] * 5
         + [pltpu.VMEM((OWN, filters.shape[1]), F32)]
         + [pltpu.VMEM(a.shape, a.dtype) for a in values]
-        + [moved] * 5
+        + [moved] * 6
+        + [pltpu.VMEM((ZS * 8, OWN, ROWS), BF)]
         + [
             pltpu.VMEM((SEQS, OWN * BLOCKS, 2 * ROWS), F32),
             pltpu.VMEM((OWN * BLOCKS, 2 * ROWS), F32),
@@ -311,34 +384,28 @@
             pltpu.VMEM((OWN * BLOCKS, 2 * ROWS), BF),
             pltpu.VMEM((OWN * BLOCKS, 2 * ROWS), BF),
             pltpu.VMEM((SEQS, OWN, taps), BF),
-            dma((5 + len(NAMES),)),
-            dma((4,)),
+            pltpu.VMEM((SEQS, OWN, taps), BF),
+            dma((8,)),
+            dma((4 + len(NAMES),)),
+            dma((5,)),
             pltpu.SemaphoreType.REGULAR,
             dma((3,)),
-            dma((3,)),
-            dma(()),
-            dma(()),
+            dma((2,)),
+            dma((4,)),
+            *[dma(())] * 6,
         ],
         compiler_params=pltpu.CompilerParams(
-            collective_id=0, has_side_effects=True, vmem_limit_bytes=56 * 1024 * 1024
+            collective_id=0, has_side_effects=True, vmem_limit_bytes=44 * 1024 * 1024
         ),
-    )(grad_out, query_proj, key_proj, value_proj, filters, *values)
-
-    steps = 4
-    block = pl.BlockSpec((1, rows, channels // steps), lambda i: (0, 0, i))
+    )(*[pltpu.with_memory_space_constraint(x, pltpu.HBM) for x in arrays])
     return pl.pallas_call(
-        finish,
-        grid=(steps,),
-        out_shape=[jax.ShapeDtypeStruct(grad_out.shape, BF)] * 3
-        + [jax.ShapeDtypeStruct((SEQS * OWN, taps), F32)],
-        in_specs=[block] * 4
-        + [
-            pl.BlockSpec((4, 2, 16 // steps, 2, OWN, ROWS), lambda i: (0, 0, i, 0, 0, 0)),
-            pl.BlockSpec((SEQS, OWN, taps // steps), lambda i: (0, 0, i)),
-        ],
-        out_specs=[block] * 3 + [pl.BlockSpec((SEQS * OWN, taps // steps), lambda i: (0, i))],
-        compiler_params=pltpu.CompilerParams(vmem_limit_bytes=32 * 1024 * 1024),
-    )(grad_out, key_proj, value_proj, conv_out, gt.reshape(4, 2, 16, 2, OWN, ROWS), fgr)
+        copy_out,
+        out_shape=[jax.ShapeDtypeStruct(x.shape, x.dtype) for x in held],
+        in_specs=[pl.BlockSpec(memory_space=pltpu.VMEM)] * 4,
+        out_specs=[any_spec] * 4,
+        scratch_shapes=[dma((4,))],
+        compiler_params=pltpu.CompilerParams(vmem_limit_bytes=16 * 1024 * 1024),
+    )(*[pltpu.with_memory_space_constraint(x, pltpu.VMEM) for x in held])
 
 
 def solution(mesh):

time: 94 us -> 87.6 us (0.932)
  Pallas kernels: 90.8 us -> 86.9 us
  local copies, waits for them, and re-layouts: 2.18 us -> 0 us
    pallas_call x2, Pallas kernels: 90.8 us -> 86.9 us  [the longest x1 85 us: local(): pl.pallas_call(body, out_shape=[pltpu.VMEM(grad_out.shape, BF)] * 3 + [pl...]
    unnamed x12 -> x0, local copies, waits for them, and re-layouts: 2.18 us -> none
where the time goes in v3:
time: 87.6 us; the launch traced here: 87.5 us
  Pallas kernels  86.9 us (99%)
    pallas_call x1, Pallas kernels, local(): pl.pallas_call(body, out_shape=[pltpu.VMEM(grad_out.shape, BF)] * 3 + [pl...  85 us
    pallas_call x1, Pallas kernels, local(): pl.pallas_call(copy_out, out_shape=[jax.ShapeDtypeStruct(x.shape, x.dtype...  1.87 us

profile of v3, /device:TPU:1, one launch (start us, length us, event | category | flops | bytes accessed | tf_op | source)
XLA Modules:
  0.0 87.5 jit_solution(14842225012978895398)
XLA Ops:
  0.6 85.0 %shard_map.183 = (bf16[1,128,4096]{2,1,0:T(8,128)(2,1)S(1)}, bf16[1,128,4096]{2,1,0:T(8,128)(2,1)S(1)}, bf16[1,128,4096]{2,1,0:T(8,128)(2,1)S(1)}, f32[64,2048]{1,0:T(8,128)S(1)}) custom-call(bf16[1,128,4096]{2,1,0:T(8,128)(2,1)} %refs_0_.1, bf16[1,128,4096]{2,1,0:T(8,128)(2,1)} %refs_1_.1, bf16[1,128,4096]{2,1,0:T(8,128)(2,1)} %refs_2_.1, ...), custom_call_target="tpu_custom_call" | custom-call | tf_op jit(solution)/shard_map/pallas_call | solution.py:369
  85.7 1.9 %shard_map.184 = (bf16[1,128,4096]{2,1,0:T(8,128)(2,1)}, bf16[1,128,4096]{2,1,0:T(8,128)(2,1)}, bf16[1,128,4096]{2,1,0:T(8,128)(2,1)}, f32[64,2048]{1,0:T(8,128)}) custom-call(bf16[1,128,4096]{2,1,0:T(8,128)(2,1)S(1)} %get-tuple-element.8.refs_0_, bf16[1,128,4096]{2,1,0:T(8,128)(2,1)S(1)} %get-tuple-element.9.refs_1_, ...), custom_call_target="tpu_custom_call" | custom-call | tf_op jit(solution)/shard_map/pallas_call | solution.py:401

commit v4 on v3

--- a/solution.py
+++ b/solution.py
@@ -92,6 +92,11 @@
         y, x, c = (py + step // 8) % 4, (px + (step // 2) % 4) % 4, (pc + step % 2) % 2
         return y * 16 + x * 4 + c, y * 8 + x * 2 + c
 
+    barrier = pltpu.get_barrier_semaphore()
+    for dpi, add, _ in column[1:]:
+        device = (dpi, py * 16 + px * 4 + pc + add)
+        pl.semaphore_signal(barrier, inc=1, device_id=device, device_id_type=MESH)
+
     first = []
     for part in range(4):
         lanes = pl.ds(pl.multiple_of((py + part) % 4 * 1024, 1024), 1024)
@@ -100,22 +105,12 @@
     for copy in first:
         copy.start()
 
-    barrier = pltpu.get_barrier_semaphore()
-    for dpi, add, _ in column[1:]:
-        device = (dpi, py * 16 + px * 4 + pc + add)
+    along_y = [(py + step) % 4 * 16 + column[0][1] for step in range(4)]
+    along_x = [(px + step) % 4 * 4 for step in range(4)]
+    cores = [pc, (pc + 1) % 2]
+    for step in range(1, PLANE):
+        device = (dp, along_y[step // 8] + (along_x[step // 2 % 4] + cores[step % 2]))
         pl.semaphore_signal(barrier, inc=1, device_id=device, device_id_type=MESH)
-
-    @pl.loop(1, PLANE)
-    def _(step):
-        device = (dp, in_plane(step)[0] + column[0][1])
-        pl.semaphore_signal(barrier, inc=1, device_id=device, device_id_type=MESH)
-
-    pairs = [(k_h.at[0], k), (v_h.at[0], v), (c_h.at[0], co)]
-    pairs.append((f_h.at[pl.ds(dp * OWN, OWN), :], filt))
-    pairs += list(zip(tables_h, tables))
-    loads = [pltpu.make_async_copy(a, b, in_sem.at[n]) for n, (a, b) in enumerate(pairs)]
-    for copy in loads:
-        copy.start()
 
     def turn(left, right, out, m):
         lanes = pl.ds(pl.multiple_of(m * 128, 128), 128)
@@ -219,6 +214,13 @@
         ).start()
     own_mid = pltpu.make_async_copy(sent_s.at[pl.ds(column[0][2] + row, 8)], mid.at[mine], self_sem.at[0])
     own_mid.start()
+    pairs = [(k_h.at[0], k), (v_h.at[0], v), (c_h.at[0], co)]
+    pairs.append((f_h.at[pl.ds(dp * OWN, OWN), :], filt))
+    pairs += list(zip(tables_h, tables))
+    loads = [pltpu.make_async_copy(a, b, in_sem.at[n]) for n, (a, b) in enumerate(pairs)]
+    for copy in loads:
+        copy.start()
+
     for part in range(1, 4):
         turn_signal(part)
     loads[0].wait()
@@ -287,7 +289,20 @@
             inverse(chunk, idt)
         gout[tiles] = xs[...].astype(BF).reshape(BLOCKS, OWN, ROWS)
 
-    exchange(2, gout, gt, lambda step: back.at[step // 8])
+    def return_tiles(begin, end, entries):
+        @pl.loop(begin, end)
+        def _(step):
+            place = in_plane(step)
+            for entry in entries:
+                tile(gout, gt, send.at[2], back.at[step // 4], entry, place)
+
+    for entry in column[1:]:
+        tile(gout, gt, send.at[2], back.at[0], entry, in_plane(0))
+    pltpu.make_async_copy(gout.at[me], gt.at[me], self_sem.at[2]).start()
+    return_tiles(1, 20, column)
+    for half in range(2):
+        return_tiles(20, PLANE, [(w, half * 2, (w * 2 + half) * PLANE) for w in range(4)])
+
     pltpu.make_async_copy(sent_p.at[me], got_p.at[me], self_sem.at[1]).wait()
     arrived(1, got_p, ZS * PLANE - 1)
 
@@ -328,28 +343,34 @@
     pltpu.make_async_copy(mid.at[pl.ds(0, 56)], mid.at[pl.ds(0, 56)], hsend).wait()
 
     pltpu.make_async_copy(gout.at[me], gt.at[me], self_sem.at[2]).wait()
-    for part in range(4):
-        count = ZS * 8 - (part == 0)
+    for part in range(8):
+        if part == 7:
+            own.wait()
+            pltpu.make_async_copy(fgr.at[pl.ds(0, SEQS - 1)], fgr.at[pl.ds(0, SEQS - 1)], frecv).wait()
+            pltpu.make_async_copy(fgs.at[pl.ds(0, SEQS - 1)], fgs.at[pl.ds(0, SEQS - 1)], fsend).wait()
+            for d in range(SEQS):
+                fg[d * OWN : (d + 1) * OWN, :] = fgr[d].astype(F32) * (1.0 / math.sqrt(SEQS * ROWS * BLOCKS))
+
+        count = ZS * 4 - (part == 0)
         pltpu.make_async_copy(gt.at[pl.ds(0, count)], gt.at[pl.ds(0, count)], back.at[part]).wait()
 
-        @pl.loop(0, 8)
+        @pl.loop(0, 4)
         def _(i):
-            m = (py + 4 - part) % 4 * 8 + i
+            m = ((py + 4 - part // 2) % 4 * 4 + (px + 8 - part % 2 * 2 - i // 2) % 4) * 2 + i % 2
             lanes = pl.ds(pl.multiple_of(m * 128, 128), 128)
             tiles = [gt[((t % 4) * 2 + m % 2) * PLANE + (m // 2) * 2 + t // 4] for t in range(8)]
             value = jnp.concatenate(tiles, axis=0).astype(F32).T
             gk[0, :, lanes] = (value * v[:, lanes].astype(F32)).astype(BF)
             gv[0, :, lanes] = (value * k[:, lanes].astype(F32)).astype(BF)
 
-    own.wait()
-    pltpu.make_async_copy(fgr.at[pl.ds(0, SEQS - 1)], fgr.at[pl.ds(0, SEQS - 1)], frecv).wait()
-    pltpu.make_async_copy(fgs.at[pl.ds(0, SEQS - 1)], fgs.at[pl.ds(0, SEQS - 1)], fsend).wait()
-    for d in range(SEQS):
-        fg[d * OWN : (d + 1) * OWN, :] = fgr[d].astype(F32) * (1.0 / math.sqrt(SEQS * ROWS * BLOCKS))
-
 
 def copy_out(*refs):
-    copies = [pltpu.make_async_copy(refs[n], refs[4 + n], refs[8].at[n]) for n in range(4)]
+    copies = []
+    for n in range(4):
+        rows = refs[n].shape[-2] // 4
+        for part in range(4):
+            span = (0,) * (n < 3) + (pl.ds(part * rows, rows),)
+            copies.append(pltpu.make_async_copy(refs[n].at[span], refs[4 + n].at[span], refs[8].at[n, part]))
     for copy in copies:
         copy.start()
     for copy in copies:
@@ -391,7 +412,7 @@
             pltpu.SemaphoreType.REGULAR,
             dma((3,)),
             dma((2,)),
-            dma((4,)),
+            dma((8,)),
             *[dma(())] * 6,
         ],
         compiler_params=pltpu.CompilerParams(
@@ -403,7 +424,7 @@
         out_shape=[jax.ShapeDtypeStruct(x.shape, x.dtype) for x in held],
         in_specs=[pl.BlockSpec(memory_space=pltpu.VMEM)] * 4,
         out_specs=[any_spec] * 4,
-        scratch_shapes=[dma((4,))],
+        scratch_shapes=[dma((4, 4))],
         compiler_params=pltpu.CompilerParams(vmem_limit_bytes=16 * 1024 * 1024),
     )(*[pltpu.with_memory_space_constraint(x, pltpu.VMEM) for x in held])
 

time: 87.6 us -> 86.8 us (level)
  Pallas kernels: 86.9 us -> 85.3 us
    pallas_call x1, Pallas kernels: 85 us -> 83.3 us  [local(): pl.pallas_call(body, out_shape=[pltpu.VMEM(grad_out.shape, BF)] * 3 + [pl...]
where the time goes in v4:
time: 86.8 us; the launch traced here: 85.9 us
  Pallas kernels  85.3 us (98%)
    pallas_call x1, Pallas kernels, local(): pl.pallas_call(body, out_shape=[pltpu.VMEM(grad_out.shape, BF)] * 3 + [pl...  83.3 us
    pallas_call x1, Pallas kernels, local(): pl.pallas_call(copy_out, out_shape=[jax.ShapeDtypeStruct(x.shape, x.dtype...  1.96 us

profile of v4, /device:TPU:1, one launch (start us, length us, event | category | flops | bytes accessed | tf_op | source)
XLA Modules:
  0.0 85.9 jit_solution(5952981961356148808)
XLA Ops:
  0.6 83.3 %shard_map.183 = (bf16[1,128,4096]{2,1,0:T(8,128)(2,1)S(1)}, bf16[1,128,4096]{2,1,0:T(8,128)(2,1)S(1)}, bf16[1,128,4096]{2,1,0:T(8,128)(2,1)S(1)}, f32[64,2048]{1,0:T(8,128)S(1)}) custom-call(bf16[1,128,4096]{2,1,0:T(8,128)(2,1)} %refs_0_.1, bf16[1,128,4096]{2,1,0:T(8,128)(2,1)} %refs_1_.1, bf16[1,128,4096]{2,1,0:T(8,128)(2,1)} %refs_2_.1, ...), custom_call_target="tpu_custom_call" | custom-call | tf_op jit(solution)/shard_map/pallas_call | solution.py:390
  84.0 2.0 %shard_map.184 = (bf16[1,128,4096]{2,1,0:T(8,128)(2,1)}, bf16[1,128,4096]{2,1,0:T(8,128)(2,1)}, bf16[1,128,4096]{2,1,0:T(8,128)(2,1)}, f32[64,2048]{1,0:T(8,128)}) custom-call(bf16[1,128,4096]{2,1,0:T(8,128)(2,1)S(1)} %get-tuple-element.8.refs_0_, bf16[1,128,4096]{2,1,0:T(8,128)(2,1)S(1)} %get-tuple-element.9.refs_1_, ...), custom_call_target="tpu_custom_call" | custom-call | tf_op jit(solution)/shard_map/pallas_call | solution.py:422
